TPU v7x, 512 devices: a whole 4x8x8 slice. The times are simulated.
512 devices in a mesh: row: 32 (over y, x_lo, core), col: 16 (over x_hi, z).
Axes of the slice: x: 4 (x_hi: 2, x_lo: 2; x = x_hi * 2 + x_lo), y: 8, z: 8, core: 2. Of those that a mesh axis runs over, the one named last changes fastest.
Arguments:
- picture_encoder_output: bfloat16 [98304, 1152], P(('row', 'col')), may hold values from -0.59765625 to 0.59765625
- caption_encoder_output: bfloat16 [98304, 1152], P(('row', 'col')), may hold values from -0.59765625 to 0.59765625
- softness_factor_exponent: float32 [], replicated, may hold values from 2.7 to 3.7
- logit_offset_term: float32 [], replicated, may hold values from -5 to -2
Outputs:
- image_grad: float32 [98304, 1152], P(('row', 'col'))
- text_grad: float32 [98304, 1152], P(('row', 'col'))
All inputs are finite; a program needn't handle non-finite values.
Results may differ from a plain program's by a relative error of at most 0.008.
Values may be sent and summed in bfloat16 or wider, within the bound.
A program may use at most 64 MiB of HBM per device.

v0:
```python
import jax
import jax.numpy as jnp
from jax import lax
from jax.sharding import PartitionSpec as P

eps_norm = 1e-06


def passed_along(value, axis, steps):
    count = lax.axis_size(axis)
    pairs = [(source, (source + steps) % count) for source in range(count)]
    return lax.ppermute(value, axis, pairs)


def unit_rows(feature):
    values = feature.astype(jnp.float32)
    inverse = lax.rsqrt(jnp.sum(values * values, axis=-1, keepdims=True) + eps_norm)
    return (values * inverse, inverse)


def unit_back(unit, inverse, direction):
    along = jnp.sum(unit * direction, axis=-1, keepdims=True)
    return inverse * (direction - unit * along)


def row_text(piece):
    return passed_along(piece, "row", 1)


def row_partial(partial_value):
    return passed_along(partial_value, "row", 1)


def row_return(partial_value, row_extent):
    return passed_along(partial_value.astype(jnp.bfloat16), "row", 1 - row_extent).astype(
        partial_value.dtype
    )


def col_text(piece):
    return passed_along(piece, "col", 1)


def col_partial(partial_value):
    return passed_along(partial_value.astype(jnp.bfloat16), "col", 1).astype(partial_value.dtype)


def col_return(partial_value, column_extent):
    return passed_along(partial_value.astype(jnp.bfloat16), "col", 1 - column_extent).astype(
        partial_value.dtype
    )


def on_device(
    picture_encoder_output, caption_encoder_output, softness_factor_exponent, logit_offset_term
):
    row_extent = min(8, lax.axis_size("row") // 2)
    column_extent = min(4, lax.axis_size("col") // 2)
    img_unit, img_inv = unit_rows(picture_encoder_output)
    txt_unit, text_inverse_norm = unit_rows(caption_encoder_output)
    img_half = img_unit.astype(jnp.bfloat16)
    txt_half = txt_unit.astype(jnp.bfloat16)
    trained_softness_factor = jnp.exp(softness_factor_exponent)
    row_count = caption_encoder_output.shape[0]
    feat_width = caption_encoder_output.shape[1]
    diagonal = jnp.eye(row_count, dtype=jnp.float32)
    empty = jnp.zeros((row_count, feat_width), jnp.float32)

    def weigh(images, texts, match_target_sign):
        matched_cosine_scores = lax.dot_general(
            images, texts, (((1,), (1,)), ((), ())), preferred_element_type=jnp.float32
        )
        return (
            trained_softness_factor
            * (
                jax.nn.sigmoid(trained_softness_factor * matched_cosine_scores + logit_offset_term)
                - match_target_sign
            )
        ).astype(jnp.bfloat16)

    def visit(piece, partial_value, img_dir, match_target_sign):
        matched_loss_multipliers = weigh(img_half, piece, match_target_sign)
        img_dir = img_dir + jnp.dot(
            matched_loss_multipliers, piece, preferred_element_type=jnp.float32
        )
        partial_value = partial_value + lax.dot_general(
            matched_loss_multipliers,
            img_half,
            (((0,), (0,)), ((), ())),
            preferred_element_type=jnp.float32,
        )
        return (partial_value, img_dir)

    first_acc, img_dir = visit(txt_half, empty, empty, diagonal)
    row_state = (txt_half, first_acc)
    col_state = (txt_half, None)
    shared = (img_dir, None)
    for step in range(1, row_extent):
        row_piece, row_acc = row_state
        row_img_dir, row_unused = shared
        row_piece = row_text(row_piece)
        row_acc = row_partial(row_acc)
        row_acc, row_img_dir = visit(row_piece, row_acc, row_img_dir, 0.0)
        row_state = (row_piece, row_acc)
        shared = (row_img_dir, row_unused)
    for step in range(1, column_extent):
        col_piece, col_acc = col_state
        col_img_dir, unused = shared
        col_piece = col_text(col_piece)
        if col_acc is None:
            col_acc = empty
        else:
            col_acc = col_partial(col_acc)
        col_acc, col_img_dir = visit(col_piece, col_acc, col_img_dir, 0.0)
        col_state = (col_piece, col_acc)
        shared = (col_img_dir, unused)
    img_dir = shared[0]
    text_dir = row_return(row_state[1], row_extent) + col_return(col_state[1], column_extent)
    return (unit_back(img_unit, img_inv, img_dir), unit_back(txt_unit, text_inverse_norm, text_dir))


def solution(mesh):
    return jax.shard_map(
        on_device,
        mesh=mesh,
        in_specs=(P(("row", "col"), None), P(("row", "col"), None), P(), P()),
        out_specs=(P(("row", "col"), None), P(("row", "col"), None)),
        check_vma=False,
    )
```

profile of v0, /device:TPU:1, one launch (start us, length us, event | category | flops | bytes accessed | tf_op | source)
XLA Modules:
  0.0 202.8 jit_solution(12142288417987637203)
XLA Ops:
  2.1 4.8 %collective-permute-start.7 = (bf16[192,1152]{1,0:T(8,128)(2,1)S(1)}, bf16[192,1152]{1,0:T(8,128)(2,1)S(1)}, u32[]{:S(2)}, u32[]{:S(2)}) collective-permute-start(bf16[192,1152]{1,0:T(8,128)(2,1)S(1)} %fusion.81), channel_id=1, source_target_pairs={{0,1},{1,2},{2,3},{3,4},{4,5},{5,6},{6,7},{7,8},{8,9},{9,10},{10,1... | collective-permute-start | bytes 1327112 | tf_op jit(solution)/shard_map/ppermute | solution.py:12
  6.9 4.0 %collective-permute-start = (bf16[192,1152]{1,0:T(8,128)(2,1)S(1)}, bf16[192,1152]{1,0:T(8,128)(2,1)S(1)}, u32[]{:S(2)}, u32[]{:S(2)}) collective-permute-start(bf16[192,1152]{1,0:T(8,128)(2,1)S(1)} %fusion.81), channel_id=1, source_target_pairs={{0,16},{16,32},{32,48},{48,64},{64,80},{80,96},{96,112},{112,128},... | collective-permute-start | bytes 1327112 | tf_op jit(solution)/shard_map/ppermute | solution.py:12
  13.2 1.9 collective-permute-start.10
  15.4 10.6 %collective-permute-done.7 = bf16[192,1152]{1,0:T(8,128)(2,1)S(1)} collective-permute-done((bf16[192,1152]{1,0:T(8,128)(2,1)S(1)}, bf16[192,1152]{1,0:T(8,128)(2,1)S(1)}, u32[]{:S(2)}, u32[]{:S(2)}) %collective-permute-start.7) | collective-permute-done | bytes 442400 | tf_op jit(solution)/shard_map/ppermute | solution.py:12
  30.6 12.8 %collective-permute-start.1 = (bf16[192,1152]{1,0:T(8,128)(2,1)S(1)}, bf16[192,1152]{1,0:T(8,128)(2,1)S(1)}, u32[]{:S(2)}, u32[]{:S(2)}) collective-permute-start(bf16[192,1152]{1,0:T(8,128)(2,1)S(1)} %collective-permute-done), channel_id=1, source_target_pairs={{0,16},{16,32},{32,48},{48,64},{64,80},{80,96},{96,112},{112,128},... | collective-permute-start | bytes 1327112 | tf_op jit(solution)/shard_map/ppermute | solution.py:12
  44.3 9.7 %collective-permute-done.10 = f32[192,1152]{1,0:T(8,128)S(1)} collective-permute-done((f32[192,1152]{1,0:T(8,128)S(1)}, f32[192,1152]{1,0:T(8,128)S(1)}, u32[]{:S(2)}, u32[]{:S(2)}) %collective-permute-start.10) | collective-permute-done | bytes 884768 | tf_op jit(solution)/shard_map/ppermute | solution.py:12
  54.4 4.4 %collective-permute-start.11 = (f32[192,1152]{1,0:T(8,128)S(1)}, f32[192,1152]{1,0:T(8,128)S(1)}, u32[]{:S(2)}, u32[]{:S(2)}) collective-permute-start(f32[192,1152]{1,0:T(8,128)S(1)} %convolution_add_fusion), channel_id=1, source_target_pairs={{0,16},{16,32},{32,48},{48,64},{64,80},{80,96},{96,112},{112,128},... | collective-permute-start | bytes 2654216 | tf_op jit(solution)/shard_map/ppermute | solution.py:12
  63.5 20.1 %collective-permute-start.2 = (bf16[192,1152]{1,0:T(8,128)(2,1)S(1)}, bf16[192,1152]{1,0:T(8,128)(2,1)S(1)}, u32[]{:S(2)}, u32[]{:S(2)}) collective-permute-start(bf16[192,1152]{1,0:T(8,128)(2,1)S(1)} %collective-permute-done.1), channel_id=1, source_target_pairs={{0,16},{16,32},{32,48},{48,64},{64,80},{80,96},{96,112},{112,128},... | collective-permute-start | bytes 1327112 | tf_op jit(solution)/shard_map/ppermute | solution.py:12
  84.6 7.8 %collective-permute-done.2 = bf16[192,1152]{1,0:T(8,128)(2,1)S(1)} collective-permute-done((bf16[192,1152]{1,0:T(8,128)(2,1)S(1)}, bf16[192,1152]{1,0:T(8,128)(2,1)S(1)}, u32[]{:S(2)}, u32[]{:S(2)}) %collective-permute-start.2) | collective-permute-done | bytes 442400 | tf_op jit(solution)/shard_map/ppermute | solution.py:12
  92.5 4.4 %collective-permute-start.3 = (bf16[192,1152]{1,0:T(8,128)(2,1)S(1)}, bf16[192,1152]{1,0:T(8,128)(2,1)S(1)}, u32[]{:S(2)}, u32[]{:S(2)}) collective-permute-start(bf16[192,1152]{1,0:T(8,128)(2,1)S(1)} %collective-permute-done.2), channel_id=1, source_target_pairs={{0,16},{16,32},{32,48},{48,64},{64,80},{80,96},{96,112},{112,128},... | collective-permute-start | bytes 1327112 | tf_op jit(solution)/shard_map/ppermute | solution.py:12
  100.4 11.1 %collective-permute-done.12 = f32[192,1152]{1,0:T(8,128)S(1)} collective-permute-done((f32[192,1152]{1,0:T(8,128)S(1)}, f32[192,1152]{1,0:T(8,128)S(1)}, u32[]{:S(2)}, u32[]{:S(2)}) %collective-permute-start.12) | collective-permute-done | bytes 884768 | tf_op jit(solution)/shard_map/ppermute | solution.py:12
  111.6 4.4 %collective-permute-start.13 = (f32[192,1152]{1,0:T(8,128)S(1)}, f32[192,1152]{1,0:T(8,128)S(1)}, u32[]{:S(2)}, u32[]{:S(2)}) collective-permute-start(f32[192,1152]{1,0:T(8,128)S(1)} %add.192), channel_id=1, source_target_pairs={{0,16},{16,32},{32,48},{48,64},{64,80},{80,96},{96,112},{112,128},... | collective-permute-start | bytes 2654216 | tf_op jit(solution)/shard_map/ppermute | solution.py:12
  118.4 1.9 collective-permute-start.4
  121.1 4.9 %collective-permute-done.13 = f32[192,1152]{1,0:T(8,128)S(1)} collective-permute-done((f32[192,1152]{1,0:T(8,128)S(1)}, f32[192,1152]{1,0:T(8,128)S(1)}, u32[]{:S(2)}, u32[]{:S(2)}) %collective-permute-start.13) | collective-permute-done | bytes 884768 | tf_op jit(solution)/shard_map/ppermute | solution.py:12
  126.1 4.4 %collective-permute-start.14 = (f32[192,1152]{1,0:T(8,128)S(1)}, f32[192,1152]{1,0:T(8,128)S(1)}, u32[]{:S(2)}, u32[]{:S(2)}) collective-permute-start(f32[192,1152]{1,0:T(8,128)S(1)} %add.193), channel_id=1, source_target_pairs={{0,16},{16,32},{32,48},{48,64},{64,80},{80,96},{96,112},{112,128},... | collective-permute-start | bytes 2654216 | tf_op jit(solution)/shard_map/ppermute | solution.py:12
  130.8 4.3 %collective-permute-start.5 = (bf16[192,1152]{1,0:T(8,128)(2,1)S(1)}, bf16[192,1152]{1,0:T(8,128)(2,1)S(1)}, u32[]{:S(2)}, u32[]{:S(2)}) collective-permute-start(bf16[192,1152]{1,0:T(8,128)(2,1)S(1)} %collective-permute-done.4), channel_id=1, source_target_pairs={{0,16},{16,32},{32,48},{48,64},{64,80},{80,96},{96,112},{112,128},... | collective-permute-start | bytes 1327112 | tf_op jit(solution)/shard_map/ppermute | solution.py:12
  136.2 4.3 %collective-permute-done.14 = f32[192,1152]{1,0:T(8,128)S(1)} collective-permute-done((f32[192,1152]{1,0:T(8,128)S(1)}, f32[192,1152]{1,0:T(8,128)S(1)}, u32[]{:S(2)}, u32[]{:S(2)}) %collective-permute-start.14) | collective-permute-done | bytes 884768 | tf_op jit(solution)/shard_map/ppermute | solution.py:12
  140.6 4.4 %collective-permute-start.15 = (f32[192,1152]{1,0:T(8,128)S(1)}, f32[192,1152]{1,0:T(8,128)S(1)}, u32[]{:S(2)}, u32[]{:S(2)}) collective-permute-start(f32[192,1152]{1,0:T(8,128)S(1)} %add.194), channel_id=1, source_target_pairs={{0,16},{16,32},{32,48},{48,64},{64,80},{80,96},{96,112},{112,128},... | collective-permute-start | bytes 2654216 | tf_op jit(solution)/shard_map/ppermute | solution.py:12
  145.6 4.4 %collective-permute-start.6 = (bf16[192,1152]{1,0:T(8,128)(2,1)S(1)}, bf16[192,1152]{1,0:T(8,128)(2,1)S(1)}, u32[]{:S(2)}, u32[]{:S(2)}) collective-permute-start(bf16[192,1152]{1,0:T(8,128)(2,1)S(1)} %collective-permute-done.5), channel_id=1, source_target_pairs={{0,16},{16,32},{32,48},{48,64},{64,80},{80,96},{96,112},{112,128},... | collective-permute-start | bytes 1327112 | tf_op jit(solution)/shard_map/ppermute | solution.py:12
  150.7 9.0 %collective-permute-done.6 = bf16[192,1152]{1,0:T(8,128)(2,1)S(1)} collective-permute-done((bf16[192,1152]{1,0:T(8,128)(2,1)S(1)}, bf16[192,1152]{1,0:T(8,128)(2,1)S(1)}, u32[]{:S(2)}, u32[]{:S(2)}) %collective-permute-start.6) | collective-permute-done | bytes 442400 | tf_op jit(solution)/shard_map/ppermute | solution.py:12
  160.2 4.4 %collective-permute-start.16 = (f32[192,1152]{1,0:T(8,128)S(1)}, f32[192,1152]{1,0:T(8,128)S(1)}, u32[]{:S(2)}, u32[]{:S(2)}) collective-permute-start(f32[192,1152]{1,0:T(8,128)S(1)} %add.195), channel_id=1, source_target_pairs={{0,16},{16,32},{32,48},{48,64},{64,80},{80,96},{96,112},{112,128},... | collective-permute-start | bytes 2654216 | tf_op jit(solution)/shard_map/ppermute | solution.py:12
  165.9 9.4 %collective-permute-done.16 = f32[192,1152]{1,0:T(8,128)S(1)} collective-permute-done((f32[192,1152]{1,0:T(8,128)S(1)}, f32[192,1152]{1,0:T(8,128)S(1)}, u32[]{:S(2)}, u32[]{:S(2)}) %collective-permute-start.16) | collective-permute-done | bytes 884768 | tf_op jit(solution)/shard_map/ppermute | solution.py:12
  175.4 7.3 %collective-permute-start.17 = (bf16[192,1152]{1,0:T(8,128)(2,1)S(1)}, bf16[192,1152]{1,0:T(8,128)(2,1)S(1)}, u32[]{:S(2)}, u32[]{:S(2)}) collective-permute-start(bf16[192,1152]{1,0:T(8,128)(2,1)S(1)} %add_convert_fusion.2), channel_id=1, source_target_pairs={{0,400},{16,416},{32,432},{48,448},{64,464},{80,480},{96,496},{112... | collective-permute-start | bytes 1327112 | tf_op jit(solution)/shard_map/ppermute | solution.py:12
  183.8 17.5 %collective-permute-done.17 = bf16[192,1152]{1,0:T(8,128)(2,1)S(1)} collective-permute-done((bf16[192,1152]{1,0:T(8,128)(2,1)S(1)}, bf16[192,1152]{1,0:T(8,128)(2,1)S(1)}, u32[]{:S(2)}, u32[]{:S(2)}) %collective-permute-start.17) | collective-permute-done | bytes 442400 | tf_op jit(solution)/shard_map/ppermute | solution.py:12
  (70 shorter events, 28.2 us)
Async XLA Ops:
  0.6 1.3 copy-start.1
  1.9 9.0 %copy-start = (bf16[192,1152]{1,0:T(8,128)(2,1)S(1)}, bf16[192,1152]{1,0:T(8,128)(2,1)}, u32[]{:S(2)}) copy-start(bf16[192,1152]{1,0:T(8,128)(2,1)} %param.4) | copy-start | bytes 1327108
  2.1 23.9 %collective-permute-start.7 = (bf16[192,1152]{1,0:T(8,128)(2,1)S(1)}, bf16[192,1152]{1,0:T(8,128)(2,1)S(1)}, u32[]{:S(2)}, u32[]{:S(2)}) collective-permute-start(bf16[192,1152]{1,0:T(8,128)(2,1)S(1)} %fusion.81), channel_id=1, source_target_pairs={{0,1},{1,2},{2,3},{3,4},{4,5},{5,6},{6,7},{7,8},{8,9},{9,10},{10,1... | collective-permute-start | bytes 1327112 | tf_op jit(solution)/shard_map/ppermute | solution.py:12
  6.9 23.7 %collective-permute-start = (bf16[192,1152]{1,0:T(8,128)(2,1)S(1)}, bf16[192,1152]{1,0:T(8,128)(2,1)S(1)}, u32[]{:S(2)}, u32[]{:S(2)}) collective-permute-start(bf16[192,1152]{1,0:T(8,128)(2,1)S(1)} %fusion.81), channel_id=1, source_target_pairs={{0,16},{16,32},{32,48},{48,64},{64,80},{80,96},{96,112},{112,128},... | collective-permute-start | bytes 1327112 | tf_op jit(solution)/shard_map/ppermute | solution.py:12
  13.2 40.8 %collective-permute-start.10 = (f32[192,1152]{1,0:T(8,128)S(1)}, f32[192,1152]{1,0:T(8,128)S(1)}, u32[]{:S(2)}, u32[]{:S(2)}) collective-permute-start(f32[192,1152]{1,0:T(8,128)S(1)} %fusion.111), channel_id=1, source_target_pairs={{0,16},{16,32},{32,48},{48,64},{64,80},{80,96},{96,112},{112,128},... | collective-permute-start | bytes 2654216 | tf_op jit(solution)/shard_map/ppermute | solution.py:12
  26.7 32.5 %collective-permute-start.18 = (bf16[192,1152]{1,0:T(8,128)(2,1)S(1)}, bf16[192,1152]{1,0:T(8,128)(2,1)S(1)}, u32[]{:S(2)}, u32[]{:S(2)}) collective-permute-start(bf16[192,1152]{1,0:T(8,128)(2,1)S(1)} %convolution_convert_fusion), channel_id=1, source_target_pairs={{0,1},{1,2},{2,3},{3,4},{4,5},{5,6},{6,7},{7,8},{8,9},{9,10},{10,1... | collective-permute-start | bytes 1327112 | tf_op jit(solution)/shard_map/ppermute | solution.py:12
  28.7 30.1 %collective-permute-start.8 = (bf16[192,1152]{1,0:T(8,128)(2,1)S(1)}, bf16[192,1152]{1,0:T(8,128)(2,1)S(1)}, u32[]{:S(2)}, u32[]{:S(2)}) collective-permute-start(bf16[192,1152]{1,0:T(8,128)(2,1)S(1)} %collective-permute-done.7), channel_id=1, source_target_pairs={{0,1},{1,2},{2,3},{3,4},{4,5},{5,6},{6,7},{7,8},{8,9},{9,10},{10,1... | collective-permute-start | bytes 1327112 | tf_op jit(solution)/shard_map/ppermute | solution.py:12
  30.6 32.9 %collective-permute-start.1 = (bf16[192,1152]{1,0:T(8,128)(2,1)S(1)}, bf16[192,1152]{1,0:T(8,128)(2,1)S(1)}, u32[]{:S(2)}, u32[]{:S(2)}) collective-permute-start(bf16[192,1152]{1,0:T(8,128)(2,1)S(1)} %collective-permute-done), channel_id=1, source_target_pairs={{0,16},{16,32},{32,48},{48,64},{64,80},{80,96},{96,112},{112,128},... | collective-permute-start | bytes 1327112 | tf_op jit(solution)/shard_map/ppermute | solution.py:12
  54.4 42.5 %collective-permute-start.11 = (f32[192,1152]{1,0:T(8,128)S(1)}, f32[192,1152]{1,0:T(8,128)S(1)}, u32[]{:S(2)}, u32[]{:S(2)}) collective-permute-start(f32[192,1152]{1,0:T(8,128)S(1)} %convolution_add_fusion), channel_id=1, source_target_pairs={{0,16},{16,32},{32,48},{48,64},{64,80},{80,96},{96,112},{112,128},... | collective-permute-start | bytes 2654216 | tf_op jit(solution)/shard_map/ppermute | solution.py:12
  59.6 56.5 %collective-permute-start.19 = (bf16[192,1152]{1,0:T(8,128)(2,1)S(1)}, bf16[192,1152]{1,0:T(8,128)(2,1)S(1)}, u32[]{:S(2)}, u32[]{:S(2)}) collective-permute-start(bf16[192,1152]{1,0:T(8,128)(2,1)S(1)} %add_convert_fusion.1), channel_id=1, source_target_pairs={{0,1},{1,2},{2,3},{3,4},{4,5},{5,6},{6,7},{7,8},{8,9},{9,10},{10,1... | collective-permute-start | bytes 1327112 | tf_op jit(solution)/shard_map/ppermute | solution.py:12
  61.5 37.4 %collective-permute-start.9 = (bf16[192,1152]{1,0:T(8,128)(2,1)S(1)}, bf16[192,1152]{1,0:T(8,128)(2,1)S(1)}, u32[]{:S(2)}, u32[]{:S(2)}) collective-permute-start(bf16[192,1152]{1,0:T(8,128)(2,1)S(1)} %collective-permute-done.8), channel_id=1, source_target_pairs={{0,1},{1,2},{2,3},{3,4},{4,5},{5,6},{6,7},{7,8},{8,9},{9,10},{10,1... | collective-permute-start | bytes 1327112 | tf_op jit(solution)/shard_map/ppermute | solution.py:12
  63.5 29.0 %collective-permute-start.2 = (bf16[192,1152]{1,0:T(8,128)(2,1)S(1)}, bf16[192,1152]{1,0:T(8,128)(2,1)S(1)}, u32[]{:S(2)}, u32[]{:S(2)}) collective-permute-start(bf16[192,1152]{1,0:T(8,128)(2,1)S(1)} %collective-permute-done.1), channel_id=1, source_target_pairs={{0,16},{16,32},{32,48},{48,64},{64,80},{80,96},{96,112},{112,128},... | collective-permute-start | bytes 1327112 | tf_op jit(solution)/shard_map/ppermute | solution.py:12
  92.5 25.9 %collective-permute-start.3 = (bf16[192,1152]{1,0:T(8,128)(2,1)S(1)}, bf16[192,1152]{1,0:T(8,128)(2,1)S(1)}, u32[]{:S(2)}, u32[]{:S(2)}) collective-permute-start(bf16[192,1152]{1,0:T(8,128)(2,1)S(1)} %collective-permute-done.2), channel_id=1, source_target_pairs={{0,16},{16,32},{32,48},{48,64},{64,80},{80,96},{96,112},{112,128},... | collective-permute-start | bytes 1327112 | tf_op jit(solution)/shard_map/ppermute | solution.py:12
  97.0 14.6 %collective-permute-start.12 = (f32[192,1152]{1,0:T(8,128)S(1)}, f32[192,1152]{1,0:T(8,128)S(1)}, u32[]{:S(2)}, u32[]{:S(2)}) collective-permute-start(f32[192,1152]{1,0:T(8,128)S(1)} %add.191), channel_id=1, source_target_pairs={{0,16},{16,32},{32,48},{48,64},{64,80},{80,96},{96,112},{112,128},... | collective-permute-start | bytes 2654216 | tf_op jit(solution)/shard_map/ppermute | solution.py:12
  111.6 14.4 %collective-permute-start.13 = (f32[192,1152]{1,0:T(8,128)S(1)}, f32[192,1152]{1,0:T(8,128)S(1)}, u32[]{:S(2)}, u32[]{:S(2)}) collective-permute-start(f32[192,1152]{1,0:T(8,128)S(1)} %add.192), channel_id=1, source_target_pairs={{0,16},{16,32},{32,48},{48,64},{64,80},{80,96},{96,112},{112,128},... | collective-permute-start | bytes 2654216 | tf_op jit(solution)/shard_map/ppermute | solution.py:12
  116.1 67.7 %collective-permute-start.20 = (bf16[192,1152]{1,0:T(8,128)(2,1)S(1)}, bf16[192,1152]{1,0:T(8,128)(2,1)S(1)}, u32[]{:S(2)}, u32[]{:S(2)}) collective-permute-start(bf16[192,1152]{1,0:T(8,128)(2,1)S(1)} %add_convert_fusion), channel_id=1, source_target_pairs={{0,13},{1,14},{2,15},{3,0},{4,1},{5,2},{6,3},{7,4},{8,5},{9,6},{10... | collective-permute-start | bytes 1327112 | tf_op jit(solution)/shard_map/ppermute | solution.py:12
  118.4 12.4 %collective-permute-start.4 = (bf16[192,1152]{1,0:T(8,128)(2,1)S(1)}, bf16[192,1152]{1,0:T(8,128)(2,1)S(1)}, u32[]{:S(2)}, u32[]{:S(2)}) collective-permute-start(bf16[192,1152]{1,0:T(8,128)(2,1)S(1)} %collective-permute-done.3), channel_id=1, source_target_pairs={{0,16},{16,32},{32,48},{48,64},{64,80},{80,96},{96,112},{112,128},... | collective-permute-start | bytes 1327112 | tf_op jit(solution)/shard_map/ppermute | solution.py:12
  126.1 14.4 %collective-permute-start.14 = (f32[192,1152]{1,0:T(8,128)S(1)}, f32[192,1152]{1,0:T(8,128)S(1)}, u32[]{:S(2)}, u32[]{:S(2)}) collective-permute-start(f32[192,1152]{1,0:T(8,128)S(1)} %add.193), channel_id=1, source_target_pairs={{0,16},{16,32},{32,48},{48,64},{64,80},{80,96},{96,112},{112,128},... | collective-permute-start | bytes 2654216 | tf_op jit(solution)/shard_map/ppermute | solution.py:12
  130.8 14.4 %collective-permute-start.5 = (bf16[192,1152]{1,0:T(8,128)(2,1)S(1)}, bf16[192,1152]{1,0:T(8,128)(2,1)S(1)}, u32[]{:S(2)}, u32[]{:S(2)}) collective-permute-start(bf16[192,1152]{1,0:T(8,128)(2,1)S(1)} %collective-permute-done.4), channel_id=1, source_target_pairs={{0,16},{16,32},{32,48},{48,64},{64,80},{80,96},{96,112},{112,128},... | collective-permute-start | bytes 1327112 | tf_op jit(solution)/shard_map/ppermute | solution.py:12
  140.6 19.5 %collective-permute-start.15 = (f32[192,1152]{1,0:T(8,128)S(1)}, f32[192,1152]{1,0:T(8,128)S(1)}, u32[]{:S(2)}, u32[]{:S(2)}) collective-permute-start(f32[192,1152]{1,0:T(8,128)S(1)} %add.194), channel_id=1, source_target_pairs={{0,16},{16,32},{32,48},{48,64},{64,80},{80,96},{96,112},{112,128},... | collective-permute-start | bytes 2654216 | tf_op jit(solution)/shard_map/ppermute | solution.py:12
  145.6 14.1 %collective-permute-start.6 = (bf16[192,1152]{1,0:T(8,128)(2,1)S(1)}, bf16[192,1152]{1,0:T(8,128)(2,1)S(1)}, u32[]{:S(2)}, u32[]{:S(2)}) collective-permute-start(bf16[192,1152]{1,0:T(8,128)(2,1)S(1)} %collective-permute-done.5), channel_id=1, source_target_pairs={{0,16},{16,32},{32,48},{48,64},{64,80},{80,96},{96,112},{112,128},... | collective-permute-start | bytes 1327112 | tf_op jit(solution)/shard_map/ppermute | solution.py:12
  160.2 15.1 %collective-permute-start.16 = (f32[192,1152]{1,0:T(8,128)S(1)}, f32[192,1152]{1,0:T(8,128)S(1)}, u32[]{:S(2)}, u32[]{:S(2)}) collective-permute-start(f32[192,1152]{1,0:T(8,128)S(1)} %add.195), channel_id=1, source_target_pairs={{0,16},{16,32},{32,48},{48,64},{64,80},{80,96},{96,112},{112,128},... | collective-permute-start | bytes 2654216 | tf_op jit(solution)/shard_map/ppermute | solution.py:12
  175.4 25.9 %collective-permute-start.17 = (bf16[192,1152]{1,0:T(8,128)(2,1)S(1)}, bf16[192,1152]{1,0:T(8,128)(2,1)S(1)}, u32[]{:S(2)}, u32[]{:S(2)}) collective-permute-start(bf16[192,1152]{1,0:T(8,128)(2,1)S(1)} %add_convert_fusion.2), channel_id=1, source_target_pairs={{0,400},{16,416},{32,432},{48,448},{64,464},{80,480},{96,496},{112... | collective-permute-start | bytes 1327112 | tf_op jit(solution)/shard_map/ppermute | solution.py:12
where the time goes:
time: 204 us; the launch traced here: 203 us
  starting transfers between devices  99.4 us (49%)
  waiting for transfers between devices  84.5 us (41%)
  matrix products  11.6 us (6%)
  other arithmetic  4.82 us (2%)
  between operations  2.49 us (1%)
    ppermute x21, starting transfers between devices, passed_along(): return lax.ppermute(value, axis, pairs)  99.4 us
    ppermute x21, waiting for transfers between devices, passed_along(): return lax.ppermute(value, axis, pairs)  84.5 us
    dot_general x11, matrix products, weigh(): lax.dot_general(images, texts, (((1,), (1,)), ((), ())), preferred_elemen...  4.2 us
    dot_general x11, matrix products, visit(): lax.dot_general(matched_loss_multipliers, img_half, (((0,), (0,)), ((), (...  4.14 us
  transfers between devices with their start and end apart: 21, of which 10 were waited for; matrix products, arithmetic and copies ran while one was open for 7% of the time, Pallas kernels for 0%

commit v1 on v0

v1 whole, which is shorter than its diff:
```python
import functools

import jax
import jax.numpy as jnp
from jax import lax
from jax.experimental import pallas as pl
from jax.experimental.pallas import tpu as pltpu
from jax.sharding import PartitionSpec as P

MESH = pl.DeviceIdType.MESH
eps_norm = 1e-06

OWN, COL = 0, 7
CHUNKS = 2


def kernel(
    n_row, n_col, scale_ref, bias_ref, txt_ref, img_ref, img_out, txt_out, raw, buf, acc, inv, send_sem, recv_sem, load_sem
):
    rows, width = txt_ref.shape
    part = rows // CHUNKS
    row, col = lax.axis_index("row"), lax.axis_index("col")
    core = lax.rem(row, 2)
    half = lax.rem(row // 2, 2)

    def at_row(offset):
        return (lax.rem(row + offset + n_row, n_row), col)

    def at_col(offset):
        return (row, lax.rem(col + offset + n_col, n_col))

    sibling = at_row(1 - 2 * core)
    partner = at_row(2 - 4 * half)
    across = at_row(6 * core - 3)

    barrier = pltpu.get_barrier_semaphore()
    peers = (at_row(4), at_row(-4), sibling, partner, across, at_col(1), at_col(-1))
    for peer in peers:
        pl.semaphore_signal(barrier, inc=1, device_id=peer, device_id_type=MESH)

    loads = [pltpu.make_async_copy(ref, raw.at[d], load_sem.at[d]) for d, ref in enumerate((txt_ref, img_ref))]
    for load in loads:
        load.start()
    for load in loads:
        load.wait()

    def normalise(d, c):
        span = pl.ds(c * part, part)
        values = raw[d, span, :].astype(jnp.float32)
        inverse = lax.rsqrt(jnp.sum(values * values, axis=-1, keepdims=True) + eps_norm)
        inv[d, span, :] = inverse
        buf[d, OWN, span, :] = (values * inverse).astype(jnp.bfloat16)

    for c in range(CHUNKS):
        for d in range(2):
            normalise(d, c)

    pl.semaphore_wait(barrier, len(peers))

    def copy(d, number, source, slot, c, target):
        span = pl.ds(c * part, part)
        return pltpu.make_async_remote_copy(
            src_ref=buf.at[d, source, span],
            dst_ref=buf.at[d, slot, span],
            send_sem=send_sem.at[d, number, c],
            recv_sem=recv_sem.at[d, slot, c],
            device_id=target,
            device_id_type=MESH,
        )

    def place(d):
        sign = 1 - 2 * d
        return sign, jnp.where(d == 0, half, 1 - half), jnp.where(d == 0, core, 1 - core)

    def first_sends(d, c):
        sign, h, e = place(d)
        copy(d, 0, OWN, COL + 1, c, at_col(sign)).start()
        copy(d, 3, OWN, 4, c, at_row(4 * sign)).start()

        @pl.when(h == 0)
        def _():
            copy(d, 5, OWN, 2, c, partner).start()

        @pl.when(e == 0)
        def _():
            copy(d, 6, OWN, 1, c, sibling).start()

    def arrived(d, slot, c):
        copy(d, 0, OWN, slot, c, sibling).wait_recv()

    def pass_on(d, slot, c):
        arrived(d, slot, c)
        sign, h, e = place(d)
        if slot == COL + 1 or slot == COL + 2:
            copy(d, slot - COL, slot, slot + 1, c, at_col(sign)).start()
        elif slot == 4:

            @pl.when(h == 1)
            def _():
                copy(d, 5, 4, 2, c, partner).start()

            @pl.when(e == 1)
            def _():
                copy(d, 6, 4, 7, c, across).start()

            copy(d, 8, 4, 5 - 2 * e, c, sibling).start()
        elif slot == 2:
            copy(d, 4, 2, 6, c, at_row(4 * sign)).start()
            copy(d, 7, 2, 3 - 2 * e, c, sibling).start()
        elif slot == 6:
            copy(d, 9, 6, 7 - 2 * e, c, sibling).start()

    for c in range(CHUNKS):
        for d in range(2):
            first_sends(d, c)

    scale = jnp.exp(jnp.full((1, rows), scale_ref[0, 0], jnp.float32))
    bias = bias_ref[0, 0]

    def meet(d, slot, on_diagonal=False):
        other = buf[d, slot]
        cosines = lax.dot_general(
            buf[1 - d, OWN], other, (((1,), (1,)), ((), ())), preferred_element_type=jnp.float32
        )
        chance = jax.nn.sigmoid(scale * cosines + bias)
        if on_diagonal:
            across_rows = lax.broadcasted_iota(jnp.int32, (rows, rows), 0)
            across_cols = lax.broadcasted_iota(jnp.int32, (rows, rows), 1)
            chance = chance - jnp.where(across_rows == across_cols, 1.0, 0.0)
        weights = (scale * chance).astype(jnp.bfloat16)
        term = jnp.dot(weights, other, preferred_element_type=jnp.float32)
        acc[d] = term if on_diagonal else acc[d] + term

    def meet_both(slot, on_diagonal=False):
        @pl.loop(0, 2)
        def _(d):
            meet(d, slot, on_diagonal)

    def both(slot, c):
        for d in range(2):
            pass_on(d, slot, c)

    def land(slot):
        for c in range(CHUNKS):
            for d in range(2):
                arrived(d, slot, c)

    meet_both(OWN, True)
    for c in range(CHUNKS):
        both(4, c)
        both(COL + 1, c)
    for c in range(CHUNKS):
        pass_on(1 - half, 2, c)
    meet_both(4)
    both(COL + 2, 0)
    pass_on(half, 2, 0)
    meet_both(COL + 1)
    pass_on(half, 2, 1)
    both(COL + 2, 1)
    land(1)
    meet_both(1)
    meet_both(2)
    land(3)
    meet_both(3)
    meet_both(COL + 2)
    both(6, 0)
    both(6, 1)
    land(5)
    meet_both(5)
    meet_both(6)
    land(7)
    meet_both(7)
    land(COL + 3)
    meet_both(COL + 3)

    for d, out in ((0, img_out), (1, txt_out)):
        inverse = inv[1 - d]
        unit = raw[1 - d].astype(jnp.float32) * inverse
        direction = acc[d]
        along = jnp.sum(unit * direction, axis=-1, keepdims=True)
        out[...] = inverse * (direction - unit * along)

    for d in range(2):
        for number in range(10):
            for c in range(CHUNKS):
                copy(d, number, OWN, 1, c, sibling).wait_send()


def on_device(n_row, n_col, picture, caption, scale_exponent, offset):
    rows, width = picture.shape
    scalar = pl.BlockSpec(memory_space=pltpu.SMEM)
    whole = pl.BlockSpec(memory_space=pl.ANY)
    out = jax.ShapeDtypeStruct((rows, width), jnp.float32)
    return pl.pallas_call(
        functools.partial(kernel, n_row, n_col),
        out_shape=(out, out),
        in_specs=[scalar, scalar, whole, whole],
        out_specs=[pl.BlockSpec(memory_space=pltpu.VMEM)] * 2,
        scratch_shapes=[
            pltpu.VMEM((2, rows, width), jnp.bfloat16),
            pltpu.VMEM((2, 11, rows, width), jnp.bfloat16),
            pltpu.VMEM((2, rows, width), jnp.float32),
            pltpu.VMEM((2, rows, 1), jnp.float32),
            pltpu.SemaphoreType.DMA((2, 10, CHUNKS)),
            pltpu.SemaphoreType.DMA((2, 11, CHUNKS)),
            pltpu.SemaphoreType.DMA((2,)),
        ],
        compiler_params=pltpu.CompilerParams(
            collective_id=0, has_side_effects=True, vmem_limit_bytes=48 << 20
        ),
    )(scale_exponent.reshape(1, 1), offset.reshape(1, 1), caption, picture)


def solution(mesh):
    return jax.shard_map(
        functools.partial(on_device, mesh.shape["row"], mesh.shape["col"]),
        mesh=mesh,
        in_specs=(P(("row", "col"), None), P(("row", "col"), None), P(), P()),
        out_specs=(P(("row", "col"), None), P(("row", "col"), None)),
        check_vma=False,
    )
```

time: 204 us -> 80.3 us (0.39)
  starting transfers between devices: 99.4 us -> 0 us
  waiting for transfers between devices: 84.5 us -> 0 us
  Pallas kernels: 0 us -> 74.3 us
  matrix products: 11.6 us -> 0 us
  other arithmetic: 4.82 us -> 0 us
  local copies, waits for them, and re-layouts: 0.01 us -> 3.84 us
    ppermute x21 -> x0, starting transfers between devices: 99.4 us -> none  [passed_along(): return lax.ppermute(value, axis, pairs)]
    ppermute x21 -> x0, waiting for transfers between devices: 84.5 us -> none  [passed_along(): return lax.ppermute(value, axis, pairs)]
    pallas_call x0 -> x1, Pallas kernels: none -> 74.3 us  [on_device(): pl.pallas_call(functools.partial(kernel, n_row, n_col), out_shape=(out, o...]
    dot_general x33 -> x0, matrix products: 11.6 us -> none  [the longest x11 4.2 us: weigh(): lax.dot_general(images, texts, (((1,), (1,)), ((), ())), preferred_elemen...]
    unnamed x4 -> x6, local copies, waits for them, and re-layouts: 0.01 us -> 3.84 us
    mul x2 -> x0, other arithmetic: 2.3 us -> none  [unit_back(): return inverse * (direction - unit * along)]
  transfers between devices with their start and end apart: 21 -> 0, of which waited for: 10 -> 0; matrix products, arithmetic and copies ran while one was open for 7% -> 0% of each run, Pallas kernels for 0% -> 0%
where the time goes in v1:
time: 80.3 us; the launch traced here: 80.1 us
  Pallas kernels  74.3 us (93%)
  local copies, waits for them, and re-layouts  3.84 us (5%)
  between operations  1.94 us (2%)
    pallas_call x1, Pallas kernels, on_device(): pl.pallas_call(functools.partial(kernel, n_row, n_col), out_shape=(out, o...  74.3 us
    unnamed x6, local copies, waits for them, and re-layouts  3.84 us

profile of v1, /device:TPU:1, one launch (start us, length us, event | category | flops | bytes accessed | tf_op | source)
XLA Modules:
  0.0 80.1 jit_solution(12908609583438756616)
XLA Ops:
  1.9 0.0 copy-start
  1.9 1.0 %copy-done = bf16[192,1152]{1,0:T(8,128)(2,1)S(1)} copy-done((bf16[192,1152]{1,0:T(8,128)(2,1)S(1)}, bf16[192,1152]{1,0:T(8,128)(2,1)}, u32[]{:S(2)}) %copy-start) | copy-done | bytes 442392
  2.9 0.0 copy-start.1
  2.9 1.0 %copy-done.1 = bf16[192,1152]{1,0:T(8,128)(2,1)S(1)} copy-done((bf16[192,1152]{1,0:T(8,128)(2,1)S(1)}, bf16[192,1152]{1,0:T(8,128)(2,1)}, u32[]{:S(2)}) %copy-start.1) | copy-done | bytes 442392
  3.9 74.3 %shard_map.59 = (f32[192,1152]{1,0:T(8,128)S(1)}, f32[192,1152]{1,0:T(8,128)S(1)}) custom-call(f32[1,1]{1,0:T(1,128)} %bitcast.2.scale_ref, f32[1,1]{1,0:T(1,128)} %bitcast.3.bias_ref, bf16[192,1152]{1,0:T(8,128)(2,1)S(1)} %copy-done, bf16[192,1152]{1,0:T(8,128)(2,1)S(1)} %copy-done.1), custom_call_target="tpu_custom_call" | custom-call | tf_op jit(solution)/shard_map/pallas_call | solution.py:194
  78.2 0.9 %copy.10 = f32[192,1152]{1,0:T(8,128)} copy(f32[192,1152]{1,0:T(8,128)S(1)} %get-tuple-element.4) | data formatting | bytes 1769472
  79.1 0.9 %copy.11 = f32[192,1152]{1,0:T(8,128)} copy(f32[192,1152]{1,0:T(8,128)S(1)} %get-tuple-element.5) | data formatting | bytes 1769472
Async XLA Ops:
  1.9 1.0 %copy-start = (bf16[192,1152]{1,0:T(8,128)(2,1)S(1)}, bf16[192,1152]{1,0:T(8,128)(2,1)}, u32[]{:S(2)}) copy-start(bf16[192,1152]{1,0:T(8,128)(2,1)} %txt_ref.1) | copy-start | bytes 1327108
  2.9 1.0 %copy-start.1 = (bf16[192,1152]{1,0:T(8,128)(2,1)S(1)}, bf16[192,1152]{1,0:T(8,128)(2,1)}, u32[]{:S(2)}) copy-start(bf16[192,1152]{1,0:T(8,128)(2,1)} %img_ref.1) | copy-start | bytes 1327108

commit v2 on v1

--- a/solution.py
+++ b/solution.py
@@ -10,7 +10,7 @@
 MESH = pl.DeviceIdType.MESH
 eps_norm = 1e-06
 
-OWN, COL = 0, 7
+OWN, COL, VIA = 0, 7, 11
 CHUNKS = 2
 
 
@@ -23,18 +23,28 @@
     core = lax.rem(row, 2)
     half = lax.rem(row // 2, 2)
 
+    def at(row_offset, col_offset):
+        return (lax.rem(row + row_offset + n_row, n_row), lax.rem(col + col_offset + n_col, n_col))
+
     def at_row(offset):
-        return (lax.rem(row + offset + n_row, n_row), col)
+        return at(offset, 0)
 
     def at_col(offset):
-        return (row, lax.rem(col + offset + n_col, n_col))
-
+        return at(0, offset)
+
+    depth = n_col // 2
+    level = lax.rem(col, depth)
+    beside = 2 - 4 * half
     sibling = at_row(1 - 2 * core)
-    partner = at_row(2 - 4 * half)
+    partner = at_row(beside)
     across = at_row(6 * core - 3)
+    turn = at(
+        jnp.where(jnp.logical_or(level == 0, level == depth - 1), beside, 0),
+        jnp.where(level == depth - 1, 1, jnp.where(level == 0, -1, depth)),
+    )
 
     barrier = pltpu.get_barrier_semaphore()
-    peers = (at_row(4), at_row(-4), sibling, partner, across, at_col(1), at_col(-1))
+    peers = (at_row(4), at_row(-4), sibling, partner, across, at_col(1), at_col(-1), turn)
     for peer in peers:
         pl.semaphore_signal(barrier, inc=1, device_id=peer, device_id_type=MESH)
 
@@ -68,20 +78,27 @@
             device_id_type=MESH,
         )
 
-    def place(d):
-        sign = 1 - 2 * d
-        return sign, jnp.where(d == 0, half, 1 - half), jnp.where(d == 0, core, 1 - core)
+    def when(*conditions):
+        return pl.when(functools.reduce(jnp.logical_and, conditions))
+
+    places = []
+    for d in range(2):
+        z = level if d == 0 else depth - 1 - level
+        places.append((1 - 2 * d, half if d == 0 else 1 - half, core if d == 0 else 1 - core, z == depth - 1, z == 0))
 
     def first_sends(d, c):
-        sign, h, e = place(d)
-        copy(d, 0, OWN, COL + 1, c, at_col(sign)).start()
+        sign, h, e, last, _ = places[d]
         copy(d, 3, OWN, 4, c, at_row(4 * sign)).start()
 
-        @pl.when(h == 0)
+        @when(jnp.logical_not(last), h == 0)
         def _():
             copy(d, 5, OWN, 2, c, partner).start()
 
-        @pl.when(e == 0)
+        @when(jnp.logical_not(last))
+        def _():
+            copy(d, 0, OWN, COL + 1, c, at_col(sign)).start()
+
+        @when(e == 0)
         def _():
             copy(d, 6, OWN, 1, c, sibling).start()
 
@@ -90,25 +107,40 @@
 
     def pass_on(d, slot, c):
         arrived(d, slot, c)
-        sign, h, e = place(d)
+        sign, h, e, last, _ = places[d]
         if slot == COL + 1 or slot == COL + 2:
             copy(d, slot - COL, slot, slot + 1, c, at_col(sign)).start()
+        elif slot == VIA:
+            copy(d, 0, VIA, COL + 1, c, turn).start()
+            copy(d, 10, VIA, 2, c, at_row(4 * sign)).start()
         elif slot == 4:
 
-            @pl.when(h == 1)
+            @when(h == 1, jnp.logical_not(last))
             def _():
                 copy(d, 5, 4, 2, c, partner).start()
 
-            @pl.when(e == 1)
+            @when(e == 1)
             def _():
                 copy(d, 6, 4, 7, c, across).start()
 
             copy(d, 8, 4, 5 - 2 * e, c, sibling).start()
         elif slot == 2:
+
+            @when(h == 1, last)
+            def _():
+                copy(d, 0, 2, COL + 1, c, turn).start()
+
             copy(d, 4, 2, 6, c, at_row(4 * sign)).start()
             copy(d, 7, 2, 3 - 2 * e, c, sibling).start()
         elif slot == 6:
             copy(d, 9, 6, 7 - 2 * e, c, sibling).start()
+
+    for c in range(CHUNKS):
+        for d in range(2):
+
+            @pl.when(places[d][3])
+            def _(d=d, c=c):
+                copy(d, 5, OWN, jnp.where(places[d][1] == 0, 2, VIA), c, partner).start()
 
     for c in range(CHUNKS):
         for d in range(2):
@@ -136,38 +168,57 @@
         def _(d):
             meet(d, slot, on_diagonal)
 
-    def both(slot, c):
-        for d in range(2):
-            pass_on(d, slot, c)
-
     def land(slot):
         for c in range(CHUNKS):
             for d in range(2):
                 arrived(d, slot, c)
 
+    def pass_if(condition, d, slot, c):
+        @pl.when(condition)
+        def _():
+            pass_on(d, slot, c)
+
     meet_both(OWN, True)
     for c in range(CHUNKS):
-        both(4, c)
-        both(COL + 1, c)
-    for c in range(CHUNKS):
-        pass_on(1 - half, 2, c)
+        for d in range(2):
+            _, h, e, last, fresh = places[d]
+            inner = jnp.logical_not(jnp.logical_or(last, fresh))
+            pass_if(jnp.logical_and(last, h == 0), d, VIA, c)
+            pass_if(jnp.logical_and(last, h == 1), d, 2, c)
+            pass_on(d, 4, c)
+            pass_if(inner, d, COL + 1, c)
+            pass_if(jnp.logical_and(inner, h == 1), d, 2, c)
+    for c in range(CHUNKS):
+        for d in range(2):
+            pass_if(places[d][3], d, COL + 1, c)
     meet_both(4)
-    both(COL + 2, 0)
-    pass_on(half, 2, 0)
+    for c in range(CHUNKS):
+        for d in range(2):
+            pass_if(places[d][4], d, COL + 1, c)
+        for d in range(2):
+            pass_if(jnp.logical_not(places[d][4]), d, COL + 2, c)
+        for d in range(2):
+            _, h, e, last, fresh = places[d]
+            pass_if(jnp.logical_or(h == 0, fresh), d, 2, c)
+            pass_if(jnp.logical_and(h == 1, jnp.logical_not(fresh)), d, 6, c)
     meet_both(COL + 1)
-    pass_on(half, 2, 1)
-    both(COL + 2, 1)
-    land(1)
-    meet_both(1)
-    meet_both(2)
-    land(3)
-    meet_both(3)
+    for c in range(CHUNKS):
+        for d in range(2):
+            pass_if(places[d][4], d, 6, c)
+            pass_if(places[d][4], d, COL + 2, c)
+        for d in range(2):
+            _, h, e, last, fresh = places[d]
+            pass_if(jnp.logical_and(h == 0, jnp.logical_not(fresh)), d, 6, c)
+        if c == 0:
+            land(1)
+            meet_both(1)
+            meet_both(2)
+            land(3)
+            meet_both(3)
     meet_both(COL + 2)
-    both(6, 0)
-    both(6, 1)
+    meet_both(6)
     land(5)
     meet_both(5)
-    meet_both(6)
     land(7)
     meet_both(7)
     land(COL + 3)
@@ -184,12 +235,17 @@
         for number in range(10):
             for c in range(CHUNKS):
                 copy(d, number, OWN, 1, c, sibling).wait_send()
+        for c in range(CHUNKS):
+
+            @when(places[d][3], places[d][1] == 0)
+            def _(d=d, c=c):
+                copy(d, 10, OWN, 1, c, sibling).wait_send()
 
 
 def on_device(n_row, n_col, picture, caption, scale_exponent, offset):
     rows, width = picture.shape
     scalar = pl.BlockSpec(memory_space=pltpu.SMEM)
-    whole = pl.BlockSpec(memory_space=pl.ANY)
+    whole = pl.BlockSpec(memory_space=pltpu.HBM)
     out = jax.ShapeDtypeStruct((rows, width), jnp.float32)
     return pl.pallas_call(
         functools.partial(kernel, n_row, n_col),
@@ -198,11 +254,11 @@
         out_specs=[pl.BlockSpec(memory_space=pltpu.VMEM)] * 2,
         scratch_shapes=[
             pltpu.VMEM((2, rows, width), jnp.bfloat16),
-            pltpu.VMEM((2, 11, rows, width), jnp.bfloat16),
+            pltpu.VMEM((2, 12, rows, width), jnp.bfloat16),
             pltpu.VMEM((2, rows, width), jnp.float32),
             pltpu.VMEM((2, rows, 1), jnp.float32),
-            pltpu.SemaphoreType.DMA((2, 10, CHUNKS)),
             pltpu.SemaphoreType.DMA((2, 11, CHUNKS)),
+            pltpu.SemaphoreType.DMA((2, 12, CHUNKS)),
             pltpu.SemaphoreType.DMA((2,)),
         ],
         compiler_params=pltpu.CompilerParams(

time: 80.3 us -> 74.8 us (0.932)
  Pallas kernels: 74.3 us -> 68.4 us
    pallas_call x1, Pallas kernels: 74.3 us -> 68.4 us  [on_device(): pl.pallas_call(functools.partial(kernel, n_row, n_col), out_shape=(out, o...]
where the time goes in v2:
time: 74.8 us; the launch traced here: 74.2 us
  Pallas kernels  68.4 us (91%)
  local copies, waits for them, and re-layouts  3.84 us (5%)
  between operations  1.94 us (3%)
    pallas_call x1, Pallas kernels, on_device(): pl.pallas_call(functools.partial(kernel, n_row, n_col), out_shape=(out, o...  68.4 us
    unnamed x6, local copies, waits for them, and re-layouts  3.84 us

profile of v2, /device:TPU:1, one launch (start us, length us, event | category | flops | bytes accessed | tf_op | source)
XLA Modules:
  0.0 74.2 jit_solution(1049640571147317684)
XLA Ops:
  1.9 0.0 copy-start
  1.9 1.0 %copy-done = bf16[192,1152]{1,0:T(8,128)(2,1)S(1)} copy-done((bf16[192,1152]{1,0:T(8,128)(2,1)S(1)}, bf16[192,1152]{1,0:T(8,128)(2,1)}, u32[]{:S(2)}) %copy-start) | copy-done | bytes 442392
  2.9 0.0 copy-start.1
  2.9 1.0 %copy-done.1 = bf16[192,1152]{1,0:T(8,128)(2,1)S(1)} copy-done((bf16[192,1152]{1,0:T(8,128)(2,1)S(1)}, bf16[192,1152]{1,0:T(8,128)(2,1)}, u32[]{:S(2)}) %copy-start.1) | copy-done | bytes 442392
  3.9 68.4 %shard_map.59 = (f32[192,1152]{1,0:T(8,128)S(1)}, f32[192,1152]{1,0:T(8,128)S(1)}) custom-call(f32[1,1]{1,0:T(1,128)} %bitcast.2.scale_ref, f32[1,1]{1,0:T(1,128)} %bitcast.3.bias_ref, bf16[192,1152]{1,0:T(8,128)(2,1)S(1)} %copy-done, bf16[192,1152]{1,0:T(8,128)(2,1)S(1)} %copy-done.1), custom_call_target="tpu_custom_call" | custom-call | tf_op jit(solution)/shard_map/pallas_call | solution.py:250
  72.4 0.9 %copy.10 = f32[192,1152]{1,0:T(8,128)} copy(f32[192,1152]{1,0:T(8,128)S(1)} %get-tuple-element.4) | data formatting | bytes 1769472
  73.3 0.9 %copy.11 = f32[192,1152]{1,0:T(8,128)} copy(f32[192,1152]{1,0:T(8,128)S(1)} %get-tuple-element.5) | data formatting | bytes 1769472
Async XLA Ops:
  1.9 1.0 %copy-start = (bf16[192,1152]{1,0:T(8,128)(2,1)S(1)}, bf16[192,1152]{1,0:T(8,128)(2,1)}, u32[]{:S(2)}) copy-start(bf16[192,1152]{1,0:T(8,128)(2,1)} %txt_ref.1) | copy-start | bytes 1327108
  2.9 1.0 %copy-start.1 = (bf16[192,1152]{1,0:T(8,128)(2,1)S(1)}, bf16[192,1152]{1,0:T(8,128)(2,1)}, u32[]{:S(2)}) copy-start(bf16[192,1152]{1,0:T(8,128)(2,1)} %img_ref.1) | copy-start | bytes 1327108

commit v3 on v2

--- a/solution.py
+++ b/solution.py
@@ -164,8 +164,7 @@
         acc[d] = term if on_diagonal else acc[d] + term
 
     def meet_both(slot, on_diagonal=False):
-        @pl.loop(0, 2)
-        def _(d):
+        for d in range(2):
             meet(d, slot, on_diagonal)
 
     def land(slot):
@@ -178,49 +177,69 @@
         def _():
             pass_on(d, slot, c)
 
+    wraps = jnp.logical_or(level == 0, level == depth - 1)
+    within = jnp.logical_not(wraps)
+
+    def on_last(slot, c, *more):
+        for d in range(2):
+            pass_if(functools.reduce(jnp.logical_and, [f(d) for f in more], places[d][3]), d, slot, c)
+
+    def on_fresh(slot, c):
+        for d in range(2):
+            pass_if(places[d][4], d, slot, c)
+
+    def near(d):
+        return places[d][1] == 0
+
+    def far(d):
+        return places[d][1] == 1
+
+    def inside(slot, c, side=None):
+        for d in range(2):
+            pass_if(within if side is None else jnp.logical_and(within, side(d)), d, slot, c)
+
     meet_both(OWN, True)
     for c in range(CHUNKS):
-        for d in range(2):
-            _, h, e, last, fresh = places[d]
-            inner = jnp.logical_not(jnp.logical_or(last, fresh))
-            pass_if(jnp.logical_and(last, h == 0), d, VIA, c)
-            pass_if(jnp.logical_and(last, h == 1), d, 2, c)
+        on_last(VIA, c, near)
+        on_last(2, c, far)
+        for d in range(2):
             pass_on(d, 4, c)
-            pass_if(inner, d, COL + 1, c)
-            pass_if(jnp.logical_and(inner, h == 1), d, 2, c)
-    for c in range(CHUNKS):
-        for d in range(2):
-            pass_if(places[d][3], d, COL + 1, c)
+        inside(COL + 1, c)
+        inside(2, c, far)
     meet_both(4)
     for c in range(CHUNKS):
-        for d in range(2):
-            pass_if(places[d][4], d, COL + 1, c)
-        for d in range(2):
-            pass_if(jnp.logical_not(places[d][4]), d, COL + 2, c)
-        for d in range(2):
-            _, h, e, last, fresh = places[d]
-            pass_if(jnp.logical_or(h == 0, fresh), d, 2, c)
-            pass_if(jnp.logical_and(h == 1, jnp.logical_not(fresh)), d, 6, c)
+        on_fresh(COL + 1, c)
+    for c in range(CHUNKS):
+        inside(COL + 2, c)
+        inside(2, c, near)
+        inside(6, c, far)
+        on_last(2, c, near)
+        on_fresh(2, c)
+        if c == 0:
+            on_last(6, 0, far)
+    for c in range(CHUNKS):
+        on_last(COL + 1, c)
     meet_both(COL + 1)
-    for c in range(CHUNKS):
-        for d in range(2):
-            pass_if(places[d][4], d, 6, c)
-            pass_if(places[d][4], d, COL + 2, c)
-        for d in range(2):
-            _, h, e, last, fresh = places[d]
-            pass_if(jnp.logical_and(h == 0, jnp.logical_not(fresh)), d, 6, c)
+    land(1)
+    meet_both(1)
+    meet_both(2)
+    for c in range(CHUNKS):
+        inside(6, c, near)
+        on_last(COL + 2, c)
         if c == 0:
-            land(1)
-            meet_both(1)
-            meet_both(2)
             land(3)
             meet_both(3)
-    meet_both(COL + 2)
+    on_last(6, 1, far)
+    for c in range(CHUNKS):
+        on_last(6, c, near)
+        on_fresh(6, c)
+        on_fresh(COL + 2, c)
     meet_both(6)
     land(5)
     meet_both(5)
     land(7)
     meet_both(7)
+    meet_both(COL + 2)
     land(COL + 3)
     meet_both(COL + 3)
 
@@ -264,7 +283,12 @@
         compiler_params=pltpu.CompilerParams(
             collective_id=0, has_side_effects=True, vmem_limit_bytes=48 << 20
         ),
-    )(scale_exponent.reshape(1, 1), offset.reshape(1, 1), caption, picture)
+    )(
+        scale_exponent.reshape(1, 1),
+        offset.reshape(1, 1),
+        pltpu.with_memory_space_constraint(caption, pltpu.HBM),
+        pltpu.with_memory_space_constraint(picture, pltpu.HBM),
+    )
 
 
 def solution(mesh):

time: 74.8 us -> 65.1 us (0.87)
  Pallas kernels: 68.4 us -> 61.2 us
  local copies, waits for them, and re-layouts: 3.84 us -> 1.83 us
    pallas_call x1, Pallas kernels: 68.4 us -> 61.2 us  [on_device(): pl.pallas_call(functools.partial(kernel, n_row, n_col), out_shape=(out, o...]
    unnamed x6 -> x2, local copies, waits for them, and re-layouts: 3.84 us -> 1.83 us
where the time goes in v3:
time: 65.1 us; the launch traced here: 64.9 us
  Pallas kernels  61.2 us (94%)
  between operations  1.93 us (3%)
  local copies, waits for them, and re-layouts  1.83 us (3%)
    pallas_call x1, Pallas kernels, on_device(): pl.pallas_call(functools.partial(kernel, n_row, n_col), out_shape=(out, o...  61.2 us
    unnamed x2, local copies, waits for them, and re-layouts  1.83 us

profile of v3, /device:TPU:1, one launch (start us, length us, event | category | flops | bytes accessed | tf_op | source)
XLA Modules:
  0.0 64.9 jit_solution(6574028183797566769)
XLA Ops:
  1.9 61.2 %shard_map.59 = (f32[192,1152]{1,0:T(8,128)S(1)}, f32[192,1152]{1,0:T(8,128)S(1)}) custom-call(f32[1,1]{1,0:T(1,128)} %bitcast.2.scale_ref, f32[1,1]{1,0:T(1,128)} %bitcast.3.bias_ref, bf16[192,1152]{1,0:T(8,128)(2,1)} %txt_ref.1, bf16[192,1152]{1,0:T(8,128)(2,1)} %img_ref.1), custom_call_target="tpu_custom_call" | custom-call | tf_op jit(solution)/shard_map/pallas_call | solution.py:269
  63.1 0.9 %copy.10 = f32[192,1152]{1,0:T(8,128)} copy(f32[192,1152]{1,0:T(8,128)S(1)} %get-tuple-element.4) | data formatting | bytes 1769472
  64.0 0.9 %copy.11 = f32[192,1152]{1,0:T(8,128)} copy(f32[192,1152]{1,0:T(8,128)S(1)} %get-tuple-element.5) | data formatting | bytes 1769472

commit v4 on v1

v4 whole, which is shorter than its diff:
```python
import functools

import jax
import jax.numpy as jnp
from jax import lax
from jax.experimental import pallas as pl
from jax.experimental.pallas import tpu as pltpu
from jax.sharding import PartitionSpec as P

MESH = pl.DeviceIdType.MESH
eps_norm = 1e-06

OWN, COL, VIA = 0, 7, 11
CHUNKS = 2
TEXT, IMAGE = 0, 1
NEAR, FAR = 0, 1


def kernel(
    n_row, n_col, scale_ref, bias_ref, txt_ref, img_ref, img_out, txt_out, raw, buf, acc, inv, send_sem, recv_sem, load_sem, open_sem
):
    rows, width = txt_ref.shape
    part = rows // CHUNKS
    row, col = lax.axis_index("row"), lax.axis_index("col")
    core = lax.rem(row, 2)
    half = lax.rem(row // 2, 2)
    depth = n_col // 2
    level = lax.rem(col, depth)
    top, bottom = level == depth - 1, level == 0

    def at(row_offset, col_offset):
        return (lax.rem(row + row_offset + n_row, n_row), lax.rem(col + col_offset + n_col, n_col))

    def at_row(offset):
        return at(offset, 0)

    def at_col(offset):
        return at(0, offset)

    beside = 2 - 4 * half
    sibling = at_row(1 - 2 * core)
    partner = at_row(beside)
    across = at_row(6 * core - 3)
    turn = at(beside, jnp.where(top, 1, -1))
    crossing = at_col(depth)
    before = level == depth - 2

    barrier = pltpu.get_barrier_semaphore()

    def greet(peer):
        pl.semaphore_signal(barrier, inc=1, device_id=peer, device_id_type=MESH)

    for peer in (at_row(4), at_row(-4), sibling, partner, across, at_col(-1)):
        greet(peer)

    @pl.when(jnp.logical_not(top))
    def _():
        greet(at_col(1))

    @pl.when(bottom)
    def _():
        greet(turn)
        greet(at_col(depth - 2))

    @pl.when(before)
    def _():
        greet(crossing)

    loads = [pltpu.make_async_copy(ref, raw.at[d], load_sem.at[d]) for d, ref in enumerate((txt_ref, img_ref))]
    for load in loads:
        load.start()
    for load in loads:
        load.wait()

    def normalise(d, c):
        span = pl.ds(c * part, part)
        values = raw[d, span, :].astype(jnp.float32)
        inverse = lax.rsqrt(jnp.sum(values * values, axis=-1, keepdims=True) + eps_norm)
        inv[d, span, :] = inverse
        buf[d, OWN, span, :] = (values * inverse).astype(jnp.bfloat16)

    for c in range(CHUNKS):
        for d in range(2):
            normalise(d, c)

    pl.semaphore_wait(barrier, 7 + jnp.where(top, 1, 0) + jnp.where(before, 2, 0) - jnp.where(bottom, 1, 0))

    @pl.when(top)
    def _():
        for peer in (at_col(1), turn):
            pl.semaphore_signal(open_sem, inc=1, device_id=peer, device_id_type=MESH)

    def copy(d, number, source, slot, c, target):
        span = pl.ds(c * part, part)
        return pltpu.make_async_remote_copy(
            src_ref=buf.at[d, source, span],
            dst_ref=buf.at[d, slot, span],
            send_sem=send_sem.at[d, number, c],
            recv_sem=recv_sem.at[d, slot, c],
            device_id=target,
            device_id_type=MESH,
        )

    def when(*conditions):
        return pl.when(functools.reduce(jnp.logical_and, conditions))

    signs = (1, -1)
    sides = (half, 1 - half)
    ends = (core, 1 - core)
    lasts = (top, bottom)

    def first_sends(d, c):
        copy(d, 3, OWN, 4, c, at_row(4 * signs[d])).start()

        @when(jnp.logical_not(lasts[d]), sides[d] == 0)
        def _():
            copy(d, 5, OWN, 2, c, partner).start()

        @when(jnp.logical_not(lasts[d]))
        def _():
            copy(d, 0, OWN, COL + 1, c, at_col(signs[d])).start()

        if d == TEXT:

            @pl.when(before)
            def _():
                copy(d, 10, OWN, VIA, c, crossing).start()

        @when(ends[d] == 0)
        def _():
            copy(d, 6, OWN, 1, c, sibling).start()

    def arrived(d, slot, c):
        copy(d, 0, OWN, slot, c, sibling).wait_recv()

    def pass_on(d, slot, c):
        arrived(d, slot, c)
        sign, h, e, last = signs[d], sides[d], ends[d], lasts[d]
        if slot == COL + 1:
            if d == TEXT:

                @pl.when(jnp.logical_not(last))
                def _():
                    copy(d, 1, slot, slot + 1, c, at_col(sign)).start()

            else:
                copy(d, 1, slot, slot + 1, c, at_col(sign)).start()
        elif slot == COL + 2:
            copy(d, 2, slot, slot + 1, c, at_col(sign)).start()
        elif slot == VIA:
            if d == TEXT:
                copy(d, 0, VIA, COL + 1, c, turn).start()
            copy(d, 10, VIA, 2, c, at_row(4 * sign)).start()
        elif slot == 4:

            @when(h == 1, jnp.logical_not(last))
            def _():
                copy(d, 5, 4, 2, c, partner).start()

            @when(e == 1)
            def _():
                copy(d, 6, 4, 7, c, across).start()

            copy(d, 8, 4, 5 - 2 * e, c, sibling).start()
        elif slot == 2:
            if d == TEXT:

                @when(h == 1, last)
                def _():
                    copy(d, 0, 2, COL + 1, c, turn).start()

            copy(d, 4, 2, 6, c, at_row(4 * sign)).start()
            copy(d, 7, 2, 3 - 2 * e, c, sibling).start()
        elif slot == 6:
            copy(d, 9, 6, 7 - 2 * e, c, sibling).start()

    for c in range(CHUNKS):
        for d in range(2):

            @pl.when(lasts[d])
            def _(d=d, c=c):
                copy(d, 5, OWN, jnp.where(sides[d] == 0, 2, VIA), c, partner).start()

    for c in range(CHUNKS):
        for d in range(2):
            first_sends(d, c)

    scale = jnp.exp(jnp.full((1, rows), scale_ref[0, 0], jnp.float32))
    bias = bias_ref[0, 0]

    def meet(slot, on_diagonal=False):
        for d in range(2):
            other = buf[d, slot]
            cosines = lax.dot_general(
                buf[1 - d, OWN], other, (((1,), (1,)), ((), ())), preferred_element_type=jnp.float32
            )
            chance = jax.nn.sigmoid(scale * cosines + bias)
            if on_diagonal:
                across_rows = lax.broadcasted_iota(jnp.int32, (rows, rows), 0)
                across_cols = lax.broadcasted_iota(jnp.int32, (rows, rows), 1)
                chance = chance - jnp.where(across_rows == across_cols, 1.0, 0.0)
            weights = (scale * chance).astype(jnp.bfloat16)
            term = jnp.dot(weights, other, preferred_element_type=jnp.float32)
            acc[d] = term if on_diagonal else acc[d] + term

    def land(slot):
        for c in range(CHUNKS):
            for d in range(2):
                arrived(d, slot, c)

    def step(last, what, *more):
        if what == "open":
            pl.semaphore_wait(open_sem, 2)
        elif what == "turn":
            (c,) = more
            copy(last, 0, jnp.where(sides[last] == 0, VIA, 2), COL + 1, c, turn).start()
        elif what == "handed":
            (c,) = more
            pl.when(sides[last] == 0)(lambda: pass_on(last, VIA, c))
            pl.when(sides[last] == 1)(lambda: pass_on(last, 2, c))
        elif what == "both":
            slot, c = more
            pass_on(0, slot, c)
            pass_on(1, slot, c)
        else:
            slot, side, c = more
            d = last if what == "last" else 1 - last
            if side is None:
                pass_on(d, slot, c)
            else:
                pl.when(sides[d] == side)(lambda: pass_on(d, slot, c))

    def at_wrap(here, last, items):
        @pl.when(here)
        def _():
            for item in items:
                step(last, *item)

    def within(items):
        @when(jnp.logical_not(top), jnp.logical_not(bottom))
        def _():
            for slot, side, c in items:
                for d in range(2):
                    if side is None:
                        pass_on(d, slot, c)
                    else:
                        pl.when(sides[d] == side)(functools.partial(pass_on, d, slot, c))
                if slot == 2 and side == 1:

                    @pl.when(before)
                    def _(c=c):
                        arrived(TEXT, VIA, c)
                        copy(TEXT, 11, VIA, COL + 2, c, at_col(2 - depth)).start()

    meet(OWN, True)
    within([(slot, side, c) for c in range(CHUNKS) for slot, side in ((4, None), (COL + 1, None), (2, 1))])
    at_wrap(bottom, IMAGE, (
            ("handed", 0),
            ("both", 4, 0),
            ("open",),
            ("turn", 0),
            ("handed", 1),
            ("turn", 1),
            ("both", 4, 1),
        ))
    at_wrap(top, TEXT, (
            ("handed", 0),
            ("both", 4, 0),
            ("handed", 1),
            ("both", 4, 1),
        ))
    meet(4)
    within([(slot, side, c) for c in range(CHUNKS) for slot, side in ((COL + 2, None), (2, 0), (6, 1))])
    at_wrap(bottom, IMAGE, (
            ("last", 2, NEAR, 0),
            ("fresh", 2, None, 0),
            ("last", 6, FAR, 0),
            ("last", 2, NEAR, 1),
            ("fresh", 2, None, 1),
            ("last", 6, FAR, 1),
            ("fresh", COL + 1, None, 0),
            ("fresh", COL + 1, None, 1),
        ))
    at_wrap(top, TEXT, (
            ("fresh", COL + 1, None, 0),
            ("fresh", COL + 1, None, 1),
            ("last", 2, NEAR, 0),
            ("fresh", 2, None, 0),
            ("last", COL + 2, None, 0),
            ("last", 6, FAR, 0),
            ("last", 2, NEAR, 1),
            ("fresh", 2, None, 1),
            ("last", COL + 2, None, 1),
            ("last", 6, FAR, 1),
            ("last", COL + 1, None, 0),
            ("last", COL + 1, None, 1),
        ))
    meet(2)
    within([(6, 0, c) for c in range(CHUNKS)])
    at_wrap(bottom, IMAGE, (
            ("fresh", 6, None, 0),
            ("fresh", 6, None, 1),
            ("last", 6, NEAR, 0),
            ("fresh", COL + 2, None, 0),
            ("last", COL + 1, None, 0),
            ("last", COL + 1, None, 1),
            ("fresh", COL + 2, None, 1),
            ("last", 6, NEAR, 1),
            ("last", COL + 2, None, 0),
            ("last", COL + 2, None, 1),
        ))
    at_wrap(top, TEXT, (
            ("fresh", 6, None, 0),
            ("fresh", COL + 2, None, 0),
            ("last", 6, NEAR, 0),
            ("fresh", 6, None, 1),
            ("fresh", COL + 2, None, 1),
            ("last", 6, NEAR, 1),
        ))
    meet(COL + 1)
    meet(6)
    for slot in (1, 3, 5, 7):
        land(slot)
        meet(slot)
    meet(COL + 2)
    land(COL + 3)
    meet(COL + 3)

    for d, out in ((0, img_out), (1, txt_out)):
        inverse = inv[1 - d]
        unit = raw[1 - d].astype(jnp.float32) * inverse
        direction = acc[d]
        along = jnp.sum(unit * direction, axis=-1, keepdims=True)
        out[...] = inverse * (direction - unit * along)

    for d in range(2):
        for number in range(12):
            for c in range(CHUNKS):

                def sent(d=d, number=number, c=c):
                    copy(d, number, OWN, 1, c, sibling).wait_send()

                handed = jnp.logical_and(lasts[d], sides[d] == 0)
                if number == 1 and d == TEXT:
                    pl.when(jnp.logical_not(top))(sent)
                elif number == 10:
                    pl.when(jnp.logical_or(handed, before) if d == TEXT else handed)(sent)
                elif number == 11:
                    if d == TEXT:
                        pl.when(before)(sent)
                else:
                    sent()


def on_device(n_row, n_col, picture, caption, scale_exponent, offset):
    rows, width = picture.shape
    scalar = pl.BlockSpec(memory_space=pltpu.SMEM)
    whole = pl.BlockSpec(memory_space=pltpu.HBM)
    out = jax.ShapeDtypeStruct((rows, width), jnp.float32)
    return pl.pallas_call(
        functools.partial(kernel, n_row, n_col),
        out_shape=(out, out),
        in_specs=[scalar, scalar, whole, whole],
        out_specs=[pl.BlockSpec(memory_space=pltpu.VMEM)] * 2,
        scratch_shapes=[
            pltpu.VMEM((2, rows, width), jnp.bfloat16),
            pltpu.VMEM((2, 12, rows, width), jnp.bfloat16),
            pltpu.VMEM((2, rows, width), jnp.float32),
            pltpu.VMEM((2, rows, 1), jnp.float32),
            pltpu.SemaphoreType.DMA((2, 12, CHUNKS)),
            pltpu.SemaphoreType.DMA((2, 12, CHUNKS)),
            pltpu.SemaphoreType.DMA((2,)),
            pltpu.SemaphoreType.REGULAR,
        ],
        compiler_params=pltpu.CompilerParams(
            collective_id=0, has_side_effects=True, vmem_limit_bytes=48 << 20
        ),
    )(
        scale_exponent.reshape(1, 1),
        offset.reshape(1, 1),
        pltpu.with_memory_space_constraint(caption, pltpu.HBM),
        pltpu.with_memory_space_constraint(picture, pltpu.HBM),
    )


def solution(mesh):
    return jax.shard_map(
        functools.partial(on_device, mesh.shape["row"], mesh.shape["col"]),
        mesh=mesh,
        in_specs=(P(("row", "col"), None), P(("row", "col"), None), P(), P()),
        out_specs=(P(("row", "col"), None), P(("row", "col"), None)),
        check_vma=False,
    )
```

time: 80.3 us -> 59.4 us (0.74)
  the two profiles are of different devices: /device:TPU:1 before, /device:TPU:86 now
where the time goes in v4:
time: 59.4 us; the launch traced here: 59.3 us
  Pallas kernels  55.5 us (93%)
  between operations  1.93 us (3%)
  local copies, waits for them, and re-layouts  1.83 us (3%)
    pallas_call x1, Pallas kernels, on_device(): pl.pallas_call(functools.partial(kernel, n_row, n_col), out_shape=(out, o...  55.5 us
    unnamed x2, local copies, waits for them, and re-layouts  1.83 us

profile of v4, /device:TPU:86, one launch (start us, length us, event | category | flops | bytes accessed | tf_op | source)
XLA Modules:
  0.0 59.3 jit_solution(4637572502678823372)
XLA Ops:
  1.9 55.5 %shard_map.59 = (f32[192,1152]{1,0:T(8,128)S(1)}, f32[192,1152]{1,0:T(8,128)S(1)}) custom-call(f32[1,1]{1,0:T(1,128)} %bitcast.2.scale_ref, f32[1,1]{1,0:T(1,128)} %bitcast.3.bias_ref, bf16[192,1152]{1,0:T(8,128)(2,1)} %txt_ref.1, bf16[192,1152]{1,0:T(8,128)(2,1)} %img_ref.1), custom_call_target="tpu_custom_call" | custom-call | tf_op jit(solution)/shard_map/pallas_call | solution.py:360
  57.4 0.9 %copy.10 = f32[192,1152]{1,0:T(8,128)} copy(f32[192,1152]{1,0:T(8,128)S(1)} %get-tuple-element.4) | data formatting | bytes 1769472
  58.3 0.9 %copy.11 = f32[192,1152]{1,0:T(8,128)} copy(f32[192,1152]{1,0:T(8,128)S(1)} %get-tuple-element.5) | data formatting | bytes 1769472

commit v5 on v4

v5 whole, which is shorter than its diff:
```python
import functools

import jax
import jax.numpy as jnp
from jax import lax
from jax.experimental import pallas as pl
from jax.experimental.pallas import tpu as pltpu
from jax.sharding import PartitionSpec as P

MESH = pl.DeviceIdType.MESH
eps_norm = 1e-06

OWN, COL, VIA = 0, 7, 11
CHUNKS = 4
TEXT, IMAGE = 0, 1
NEAR, FAR = 0, 1


def kernel(
    n_row, n_col, scale_ref, bias_ref, txt_ref, img_ref, img_out, txt_out, raw, buf, acc, inv, send_sem, recv_sem, load_sem, open_sem
):
    rows, width = txt_ref.shape
    part = rows // CHUNKS
    row, col = lax.axis_index("row"), lax.axis_index("col")
    core = lax.rem(row, 2)
    half = lax.rem(row // 2, 2)
    depth = n_col // 2
    level = lax.rem(col, depth)
    top, bottom = level == depth - 1, level == 0

    def at(row_offset, col_offset):
        return (lax.rem(row + row_offset + n_row, n_row), lax.rem(col + col_offset + n_col, n_col))

    def at_row(offset):
        return at(offset, 0)

    def at_col(offset):
        return at(0, offset)

    beside = 2 - 4 * half
    sibling = at_row(1 - 2 * core)
    partner = at_row(beside)
    across = at_row(6 * core - 3)
    turn = at(beside, jnp.where(top, 1, -1))
    crossing = at_col(depth)
    befores = (level == depth - 2, level == 1)

    barrier = pltpu.get_barrier_semaphore()

    def greet(peer):
        pl.semaphore_signal(barrier, inc=1, device_id=peer, device_id_type=MESH)

    for peer in (at_row(4), at_row(-4), sibling, partner, across, at_col(-1)):
        greet(peer)

    @pl.when(jnp.logical_not(top))
    def _():
        greet(at_col(1))

    @pl.when(bottom)
    def _():
        greet(turn)

    @pl.when(level < 2)
    def _():
        greet(at_col(depth - 2))

    @pl.when(jnp.logical_or(*befores))
    def _():
        greet(crossing)

    def load(d, c):
        span = pl.ds(c * part, part)
        return pltpu.make_async_copy((txt_ref, img_ref)[d].at[span], raw.at[d, span], load_sem.at[d, c])

    for d in range(2):
        for c in range(CHUNKS):
            load(d, c).start()

    def normalise(d, c):
        load(d, c).wait()
        span = pl.ds(c * part, part)
        values = raw[d, span, :].astype(jnp.float32)
        inverse = lax.rsqrt(jnp.sum(values * values, axis=-1, keepdims=True) + eps_norm)
        inv[d, span, :] = inverse
        buf[d, OWN, span, :] = (values * inverse).astype(jnp.bfloat16)

    for c in range(CHUNKS):
        normalise(TEXT, c)

    pl.semaphore_wait(barrier, 7 + jnp.where(level >= depth - 2, 2, 0) + jnp.where(level == 1, 1, 0) - jnp.where(bottom, 1, 0))

    @pl.when(top)
    def _():
        for peer in (at_col(1), turn, at_col(2 - depth)):
            pl.semaphore_signal(open_sem, inc=1, device_id=peer, device_id_type=MESH)

    def copy(d, number, source, slot, c, target):
        span = pl.ds(c * part, part)
        return pltpu.make_async_remote_copy(
            src_ref=buf.at[d, source, span],
            dst_ref=buf.at[d, slot, span],
            send_sem=send_sem.at[d, number, c],
            recv_sem=recv_sem.at[d, slot, c],
            device_id=target,
            device_id_type=MESH,
        )

    def when(*conditions):
        return pl.when(functools.reduce(jnp.logical_and, conditions))

    signs = (1, -1)
    sides = (half, 1 - half)
    ends = (core, 1 - core)
    lasts = (top, bottom)

    def first_sends(d, c):
        copy(d, 3, OWN, 4, c, at_row(4 * signs[d])).start()

        @when(jnp.logical_not(lasts[d]), sides[d] == 0)
        def _():
            copy(d, 5, OWN, 2, c, partner).start()

        @when(jnp.logical_not(lasts[d]))
        def _():
            copy(d, 0, OWN, COL + 1, c, at_col(signs[d])).start()

        @pl.when(befores[d])
        def _():
            copy(d, 10, OWN, VIA, c, crossing).start()

        @when(ends[d] == 0)
        def _():
            copy(d, 6, OWN, 1, c, sibling).start()

    def arrived(d, slot, c):
        copy(d, 0, OWN, slot, c, sibling).wait_recv()

    def forward(d, slot, c):
        sign, h, e, last = signs[d], sides[d], ends[d], lasts[d]
        if slot == COL + 1:

            @pl.when(jnp.logical_not(last))
            def _():
                copy(d, 1, slot, slot + 1, c, at_col(sign)).start()

        elif slot == COL + 2:
            copy(d, 2, slot, slot + 1, c, at_col(sign)).start()
        elif slot == VIA:
            if d == TEXT:
                copy(d, 0, VIA, COL + 1, c, turn).start()
            copy(d, 10, VIA, 2, c, at_row(4 * sign)).start()
        elif slot == 4:

            @when(h == 1, jnp.logical_not(last))
            def _():
                copy(d, 5, 4, 2, c, partner).start()

            @when(e == 1)
            def _():
                copy(d, 6, 4, 7, c, across).start()

            copy(d, 8, 4, 5 - 2 * e, c, sibling).start()
        elif slot == 2:
            if d == TEXT:

                @when(h == 1, last)
                def _():
                    copy(d, 0, 2, COL + 1, c, turn).start()

            copy(d, 4, 2, 6, c, at_row(4 * sign)).start()
            copy(d, 7, 2, 3 - 2 * e, c, sibling).start()
        elif slot == 6:
            copy(d, 9, 6, 7 - 2 * e, c, sibling).start()

    def hand_over(d):
        @pl.when(lasts[d])
        def _():
            for c in range(CHUNKS):
                copy(d, 5, OWN, jnp.where(sides[d] == 0, 2, VIA), c, partner).start()

    hand_over(TEXT)
    for c in range(CHUNKS):
        normalise(IMAGE, c)
    hand_over(IMAGE)
    for c in range(CHUNKS):
        for d in range(2):
            first_sends(d, c)

    scale = jnp.exp(jnp.full((1, rows), scale_ref[0, 0], jnp.float32))
    bias = bias_ref[0, 0]

    def meet(slot, directions=(TEXT, IMAGE), on_diagonal=False):
        for d in directions:
            other = buf[d, slot]
            cosines = lax.dot_general(
                buf[1 - d, OWN], other, (((1,), (1,)), ((), ())), preferred_element_type=jnp.float32
            )
            chance = jax.nn.sigmoid(scale * cosines + bias)
            if on_diagonal:
                across_rows = lax.broadcasted_iota(jnp.int32, (rows, rows), 0)
                across_cols = lax.broadcasted_iota(jnp.int32, (rows, rows), 1)
                chance = chance - jnp.where(across_rows == across_cols, 1.0, 0.0)
            weights = (scale * chance).astype(jnp.bfloat16)
            term = jnp.dot(weights, other, preferred_element_type=jnp.float32)
            acc[d] = term if on_diagonal else acc[d] + term

    pieces = (range(CHUNKS // 2), range(CHUNKS // 2, CHUNKS))

    def see(d, slot):
        for c in range(CHUNKS):
            arrived(d, slot, c)

    def land(slot):
        see(TEXT, slot)
        see(IMAGE, slot)

    def pass_on(d, slot, piece, side=None, wait=True):
        def run():
            for c in pieces[piece]:
                if wait:
                    arrived(d, slot, c)
                forward(d, slot, c)

        if side is None:
            run()
        else:
            pl.when(sides[d] == side)(run)

    def pass_both(slot, piece, side=None):
        pass_on(TEXT, slot, piece, side)
        pass_on(IMAGE, slot, piece, side)

    def handed(d, piece):
        pass_on(d, VIA, piece, NEAR)
        pass_on(d, 2, piece, FAR)

    def cross(d, piece):
        if d == IMAGE and piece == 0:
            pl.semaphore_wait(open_sem, 1)
        for c in pieces[piece]:
            arrived(d, VIA, c)
            copy(d, 11, VIA, COL + 2, c, at_col(signs[d] * (2 - depth))).start()

    def turn_back(piece):
        for c in pieces[piece]:
            copy(IMAGE, 0, jnp.where(sides[IMAGE] == 0, VIA, 2), COL + 1, c, turn).start()

    def finish(d):
        see(d, COL + 3)
        meet(COL + 3, (d,))
        inverse = inv[1 - d]
        unit = raw[1 - d].astype(jnp.float32) * inverse
        direction = acc[d]
        along = jnp.sum(unit * direction, axis=-1, keepdims=True)
        (img_out, txt_out)[d][...] = inverse * (direction - unit * along)

    meet(OWN, on_diagonal=True)

    @when(jnp.logical_not(top), jnp.logical_not(bottom))
    def _():
        for piece in range(2):
            pass_both(4, piece)
            pass_both(COL + 1, piece)
            pass_both(2, piece, FAR)
            for d in range(2):
                pl.when(befores[d])(functools.partial(cross, d, piece))
        meet(4)
        meet(COL + 1)
        for piece in range(2):
            pass_both(COL + 2, piece)
            pass_both(2, piece, NEAR)
            pass_both(6, piece, FAR)
        meet(COL + 2)
        meet(2)
        land(3)
        meet(3)
        pass_both(6, 0, NEAR)
        land(1)
        meet(1)
        pass_both(6, 1, NEAR)
        meet(6)
        for slot in (5, 7):
            land(slot)
            meet(slot)
        finish(TEXT)
        finish(IMAGE)

    @pl.when(bottom)
    def _():
        handed(IMAGE, 0)
        pass_both(4, 0)
        pl.semaphore_wait(open_sem, 2)
        turn_back(0)
        handed(IMAGE, 1)
        turn_back(1)
        pass_both(4, 1)
        meet(4)
        see(IMAGE, COL + 1)
        meet(COL + 1, (IMAGE,))
        pass_on(IMAGE, 2, 0, NEAR)
        pass_on(TEXT, 2, 0)
        pass_on(IMAGE, 6, 0, FAR)
        pass_on(TEXT, COL + 1, 0)
        pass_on(IMAGE, 2, 1, NEAR)
        pass_on(TEXT, 2, 1)
        pass_on(IMAGE, 6, 1, FAR)
        pass_on(TEXT, COL + 1, 1)
        meet(2)
        pass_on(TEXT, 6, 0)
        meet(COL + 1, (TEXT,))
        pass_on(TEXT, 6, 1)
        meet(6, (TEXT,))
        pass_on(IMAGE, COL + 2, 0)
        pass_on(IMAGE, COL + 2, 1)
        pass_on(IMAGE, 6, 0, NEAR)
        pass_on(TEXT, COL + 2, 0)
        land(3)
        meet(3)
        meet(COL + 2, (IMAGE,))
        pass_on(IMAGE, 6, 1, NEAR)
        land(1)
        meet(1)
        pass_on(TEXT, COL + 2, 1)
        meet(6, (IMAGE,))
        meet(COL + 2, (TEXT,))
        for slot in (5, 7):
            land(slot)
            meet(slot)
        finish(IMAGE)
        finish(TEXT)

    @pl.when(top)
    def _():
        for piece in range(2):
            handed(TEXT, piece)
            pass_both(4, piece)
        meet(4)
        see(TEXT, COL + 1)
        meet(COL + 1, (TEXT,))
        pass_on(IMAGE, COL + 1, 0)
        pass_on(IMAGE, COL + 1, 1)
        for piece in range(2):
            pass_on(TEXT, 2, piece, NEAR)
            pass_on(IMAGE, 2, piece)
            pass_on(TEXT, COL + 2, piece)
            pass_on(TEXT, 6, piece, FAR)
        meet(COL + 1, (IMAGE,))
        meet(2)
        meet(COL + 2, (TEXT,))
        pass_on(IMAGE, 6, 0)
        pass_on(IMAGE, COL + 2, 0)
        land(3)
        meet(3)
        pass_on(TEXT, 6, 0, NEAR)
        pass_on(IMAGE, 6, 1)
        pass_on(IMAGE, COL + 2, 1)
        land(1)
        meet(1)
        pass_on(TEXT, 6, 1, NEAR)
        meet(6)
        meet(COL + 2, (IMAGE,))
        for slot in (5, 7):
            land(slot)
            meet(slot)
        finish(TEXT)
        finish(IMAGE)

    for d in range(2):
        for number in range(12):
            for c in range(CHUNKS):

                def sent(d=d, number=number, c=c):
                    copy(d, number, OWN, 1, c, sibling).wait_send()

                handed = jnp.logical_and(lasts[d], sides[d] == 0)
                if number == 1:
                    pl.when(jnp.logical_not(lasts[d]))(sent)
                elif number == 10:
                    pl.when(jnp.logical_or(handed, befores[d]))(sent)
                elif number == 11:
                    pl.when(befores[d])(sent)
                else:
                    sent()


def on_device(n_row, n_col, picture, caption, scale_exponent, offset):
    rows, width = picture.shape
    scalar = pl.BlockSpec(memory_space=pltpu.SMEM)
    whole = pl.BlockSpec(memory_space=pltpu.HBM)
    out = jax.ShapeDtypeStruct((rows, width), jnp.float32)
    return pl.pallas_call(
        functools.partial(kernel, n_row, n_col),
        out_shape=(out, out),
        in_specs=[scalar, scalar, whole, whole],
        out_specs=[pl.BlockSpec(memory_space=pltpu.VMEM)] * 2,
        scratch_shapes=[
            pltpu.VMEM((2, rows, width), jnp.bfloat16),
            pltpu.VMEM((2, 12, rows, width), jnp.bfloat16),
            pltpu.VMEM((2, rows, width), jnp.float32),
            pltpu.VMEM((2, rows, 1), jnp.float32),
            pltpu.SemaphoreType.DMA((2, 12, CHUNKS)),
            pltpu.SemaphoreType.DMA((2, 12, CHUNKS)),
            pltpu.SemaphoreType.DMA((2, CHUNKS)),
            pltpu.SemaphoreType.REGULAR,
        ],
        compiler_params=pltpu.CompilerParams(
            collective_id=0, has_side_effects=True, vmem_limit_bytes=48 << 20
        ),
    )(
        scale_exponent.reshape(1, 1),
        offset.reshape(1, 1),
        pltpu.with_memory_space_constraint(caption, pltpu.HBM),
        pltpu.with_memory_space_constraint(picture, pltpu.HBM),
    )


def solution(mesh):
    return jax.shard_map(
        functools.partial(on_device, mesh.shape["row"], mesh.shape["col"]),
        mesh=mesh,
        in_specs=(P(("row", "col"), None), P(("row", "col"), None), P(), P()),
        out_specs=(P(("row", "col"), None), P(("row", "col"), None)),
        check_vma=False,
    )
```

time: 59.4 us -> 57.6 us (0.970)
  the two profiles are of different devices: /device:TPU:86 before, /device:TPU:1 now
where the time goes in v5:
time: 57.6 us; the launch traced here: 57.5 us
  Pallas kernels  53.7 us (93%)
  between operations  1.93 us (3%)
  local copies, waits for them, and re-layouts  1.83 us (3%)
    pallas_call x1, Pallas kernels, on_device(): pl.pallas_call(functools.partial(kernel, n_row, n_col), out_shape=(out, o...  53.7 us
    unnamed x2, local copies, waits for them, and re-layouts  1.83 us

profile of v5, /device:TPU:1, one launch (start us, length us, event | category | flops | bytes accessed | tf_op | source)
XLA Modules:
  0.0 57.5 jit_solution(6162886385913332111)
XLA Ops:
  1.9 53.7 %shard_map.59 = (f32[192,1152]{1,0:T(8,128)S(1)}, f32[192,1152]{1,0:T(8,128)S(1)}) custom-call(f32[1,1]{1,0:T(1,128)} %bitcast.2.scale_ref, f32[1,1]{1,0:T(1,128)} %bitcast.3.bias_ref, bf16[192,1152]{1,0:T(8,128)(2,1)} %txt_ref.1, bf16[192,1152]{1,0:T(8,128)(2,1)} %img_ref.1), custom_call_target="tpu_custom_call" | custom-call | tf_op jit(solution)/shard_map/pallas_call | solution.py:392
  55.6 0.9 %copy.10 = f32[192,1152]{1,0:T(8,128)} copy(f32[192,1152]{1,0:T(8,128)S(1)} %get-tuple-element.4) | data formatting | bytes 1769472
  56.6 0.9 %copy.11 = f32[192,1152]{1,0:T(8,128)} copy(f32[192,1152]{1,0:T(8,128)S(1)} %get-tuple-element.5) | data formatting | bytes 1769472

commit v6 on v5

--- a/solution.py
+++ b/solution.py
@@ -125,9 +125,11 @@
         def _():
             copy(d, 0, OWN, COL + 1, c, at_col(signs[d])).start()
 
-        @pl.when(befores[d])
-        def _():
-            copy(d, 10, OWN, VIA, c, crossing).start()
+        if d == IMAGE:
+
+            @pl.when(befores[d])
+            def _():
+                copy(d, 10, OWN, VIA, c, crossing).start()
 
         @when(ends[d] == 0)
         def _():
@@ -180,6 +182,12 @@
                 copy(d, 5, OWN, jnp.where(sides[d] == 0, 2, VIA), c, partner).start()
 
     hand_over(TEXT)
+
+    @pl.when(befores[TEXT])
+    def _():
+        for c in range(CHUNKS):
+            copy(TEXT, 10, OWN, VIA, c, crossing).start()
+
     for c in range(CHUNKS):
         normalise(IMAGE, c)
     hand_over(IMAGE)
@@ -261,10 +269,10 @@
     def _():
         for piece in range(2):
             pass_both(4, piece)
+            pl.when(befores[TEXT])(functools.partial(cross, TEXT, piece))
             pass_both(COL + 1, piece)
             pass_both(2, piece, FAR)
-            for d in range(2):
-                pl.when(befores[d])(functools.partial(cross, d, piece))
+            pl.when(befores[IMAGE])(functools.partial(cross, IMAGE, piece))
         meet(4)
         meet(COL + 1)
         for piece in range(2):
@@ -319,10 +327,10 @@
         meet(3)
         meet(COL + 2, (IMAGE,))
         pass_on(IMAGE, 6, 1, NEAR)
+        meet(6, (IMAGE,))
         land(1)
         meet(1)
         pass_on(TEXT, COL + 2, 1)
-        meet(6, (IMAGE,))
         meet(COL + 2, (TEXT,))
         for slot in (5, 7):
             land(slot)

time: 57.6 us -> 56.1 us (0.974); the launches traced: 57.5 us -> 55.3 us
  Pallas kernels: 53.7 us -> 51.5 us
    pallas_call x1, Pallas kernels: 53.7 us -> 51.5 us  [on_device(): pl.pallas_call(functools.partial(kernel, n_row, n_col), out_shape=(out, o...]
where the time goes in v6:
time: 56.1 us; the launch traced here: 55.3 us
  Pallas kernels  51.5 us (92%)
  between operations  1.93 us (3%)
  local copies, waits for them, and re-layouts  1.83 us (3%)
    pallas_call x1, Pallas kernels, on_device(): pl.pallas_call(functools.partial(kernel, n_row, n_col), out_shape=(out, o...  51.5 us
    unnamed x2, local copies, waits for them, and re-layouts  1.83 us

profile of v6, /device:TPU:1, one launch (start us, length us, event | category | flops | bytes accessed | tf_op | source)
XLA Modules:
  0.0 55.3 jit_solution(18438965707603521110)
XLA Ops:
  1.9 51.5 %shard_map.59 = (f32[192,1152]{1,0:T(8,128)S(1)}, f32[192,1152]{1,0:T(8,128)S(1)}) custom-call(f32[1,1]{1,0:T(1,128)} %bitcast.2.scale_ref, f32[1,1]{1,0:T(1,128)} %bitcast.3.bias_ref, bf16[192,1152]{1,0:T(8,128)(2,1)} %txt_ref.1, bf16[192,1152]{1,0:T(8,128)(2,1)} %img_ref.1), custom_call_target="tpu_custom_call" | custom-call | tf_op jit(solution)/shard_map/pallas_call | solution.py:400
  53.5 0.9 %copy.10 = f32[192,1152]{1,0:T(8,128)} copy(f32[192,1152]{1,0:T(8,128)S(1)} %get-tuple-element.4) | data formatting | bytes 1769472
  54.4 0.9 %copy.11 = f32[192,1152]{1,0:T(8,128)} copy(f32[192,1152]{1,0:T(8,128)S(1)} %get-tuple-element.5) | data formatting | bytes 1769472

commit v7 on v6

--- a/solution.py
+++ b/solution.py
@@ -188,12 +188,21 @@
         for c in range(CHUNKS):
             copy(TEXT, 10, OWN, VIA, c, crossing).start()
 
+    @pl.when(top)
+    def _():
+        for c in range(CHUNKS):
+            first_sends(TEXT, c)
+
     for c in range(CHUNKS):
         normalise(IMAGE, c)
     hand_over(IMAGE)
     for c in range(CHUNKS):
-        for d in range(2):
-            first_sends(d, c)
+
+        @pl.when(jnp.logical_not(top))
+        def _(c=c):
+            first_sends(TEXT, c)
+
+        first_sends(IMAGE, c)
 
     scale = jnp.exp(jnp.full((1, rows), scale_ref[0, 0], jnp.float32))
     bias = bias_ref[0, 0]
@@ -350,8 +359,8 @@
         pass_on(IMAGE, COL + 1, 1)
         for piece in range(2):
             pass_on(TEXT, 2, piece, NEAR)
+            pass_on(TEXT, COL + 2, piece)
             pass_on(IMAGE, 2, piece)
-            pass_on(TEXT, COL + 2, piece)
             pass_on(TEXT, 6, piece, FAR)
         meet(COL + 1, (IMAGE,))
         meet(2)

time: 56.1 us -> 56.1 us (level)
  no operation moved by 1% of the time
where the time goes in v7:
time: 56.1 us; the launch traced here: 55.3 us
  Pallas kernels  51.5 us (92%)
  between operations  1.93 us (3%)
  local copies, waits for them, and re-layouts  1.83 us (3%)
    pallas_call x1, Pallas kernels, on_device(): pl.pallas_call(functools.partial(kernel, n_row, n_col), out_shape=(out, o...  51.5 us
    unnamed x2, local copies, waits for them, and re-layouts  1.83 us

profile of v7, /device:TPU:1, one launch (start us, length us, event | category | flops | bytes accessed | tf_op | source)
XLA Modules:
  0.0 55.3 jit_solution(2665576940247759521)
XLA Ops:
  1.9 51.5 %shard_map.59 = (f32[192,1152]{1,0:T(8,128)S(1)}, f32[192,1152]{1,0:T(8,128)S(1)}) custom-call(f32[1,1]{1,0:T(1,128)} %bitcast.2.scale_ref, f32[1,1]{1,0:T(1,128)} %bitcast.3.bias_ref, bf16[192,1152]{1,0:T(8,128)(2,1)} %txt_ref.1, bf16[192,1152]{1,0:T(8,128)(2,1)} %img_ref.1), custom_call_target="tpu_custom_call" | custom-call | tf_op jit(solution)/shard_map/pallas_call | solution.py:409
  53.5 0.9 %copy.10 = f32[192,1152]{1,0:T(8,128)} copy(f32[192,1152]{1,0:T(8,128)S(1)} %get-tuple-element.4) | data formatting | bytes 1769472
  54.4 0.9 %copy.11 = f32[192,1152]{1,0:T(8,128)} copy(f32[192,1152]{1,0:T(8,128)S(1)} %get-tuple-element.5) | data formatting | bytes 1769472
